TPU v7x, 32 devices: a whole 2x2x4 slice. The times are simulated.
32 devices in a mesh: gx: 4 (over y, x), gy: 8 (over z, core).
Axes of the slice: x: 2, y: 2, z: 4, core: 2. Of those that a mesh axis runs over, the one named last changes fastest.
Arguments:
- densities: bfloat16 [16, 131072], P(None, ('gx', 'gy')), may hold values from -6 to 6
- points: float32 [3, 131072], P(None, ('gx', 'gy')), may hold values from 0 to 1
- weights: float32 [131072], P(('gx', 'gy')), may hold values from 0.03 to 0.6
- near_offsets: int32 [1024, 13], P(('gx', 'gy')), may hold values from -8 to 8, as said below
- leaf_basis: bfloat16 [1024, 64, 128], P(('gx', 'gy')), may hold values from -0.5 to 0.5
- transfer: bfloat16 [1024, 64, 64], P(('gx', 'gy')), may hold values from -0.75 to 0.75
- send_lists: int32 [32, 17, 16], P(('gx', 'gy')), may hold values from 0 to 31
- relay_refs: int32 [1024, 32], P(('gx', 'gy')), may hold values from 0 to 271, as said below
- leaf_coupling: bfloat16 [1024, 32, 64, 64], P(('gx', 'gy')), may hold values from -0.25 to 0.25
- coarse_refs: int32 [128, 32], P(('gx', 'gy')), may hold values from 0 to 127
- coarse_coupling: bfloat16 [128, 32, 64, 64], P(('gx', 'gy')), may hold values from -0.125 to 0.125
Outputs:
- potential: float32 [16, 131072], P(None, ('gx', 'gy'))
Inputs may be any that keep to these rules, and one draw needn't show every extreme that they name: `near_offsets`: each leaf's offsets are distinct and the first is 0; a partner outside the leaves contributes nothing. `relay_refs`: a value never names an owner l // 32 + value // 16 - 8 outside 0 to 31; within the rows of each device's 32 leaves every other value is used at least once.
All inputs are finite; a program needn't handle non-finite values.
Results may differ from a plain program's by a relative error of at most 0.0065.
Values may be sent and summed in bfloat16 or wider, within the bound.
A program may use at most 128 MiB of HBM per device.

v0:
```python
import math

import jax
import jax.numpy as jnp
from jax import lax
from jax.sharding import PartitionSpec as P

REACH = 8
WINDOW = 8


core_square = 0.0004
four_pi = 4.0 * math.pi


def from_behind(shard, axis, by):
    devices = lax.axis_size(axis)
    pairs = [(i, i + by) for i in range(devices) if 0 <= i + by < devices]
    return lax.ppermute(shard, axis, pairs)


def near_field(densities, points, weights, near_offsets):
    rhs_count = densities.shape[0]
    leaf_count = near_offsets.shape[0]
    leaf_size = densities.shape[1] // leaf_count
    packed = jnp.concatenate([densities.astype(jnp.float32), points, weights[None, :]], axis=0)
    rim_cells = REACH * leaf_size
    from_below = from_behind(packed[:, -rim_cells:].astype(jnp.bfloat16), ("gx", "gy"), 1).astype(
        jnp.float32
    )
    from_above = from_behind(packed[:, :rim_cells], ("gx", "gy"), -1)
    extended = jnp.concatenate([from_below, packed, from_above], axis=1).reshape(
        rhs_count + 4, leaf_count + 2 * REACH, leaf_size
    )
    row_points = points.reshape(3, leaf_count, leaf_size)
    partners = jnp.arange(leaf_count, dtype=jnp.int32)[:, None] + REACH + near_offsets

    def near_block(block_index):
        partner_rows = lax.dynamic_slice_in_dim(partners, block_index * 8, 8, 0)
        partner_data = jnp.take(extended, partner_rows, axis=1)
        own_points = lax.dynamic_slice_in_dim(row_points, block_index * 8, 8, 1)
        distance = jnp.zeros((8, leaf_size, partner_rows.shape[1], leaf_size), jnp.float32)
        for component in range(3):
            offset_part = (
                own_points[component][:, :, None, None]
                - partner_data[rhs_count + component][:, None, :, :]
            )
            distance = distance + offset_part * offset_part
        kernel = (
            partner_data[rhs_count + 3][:, None, :, :]
            / (four_pi * jnp.sqrt(distance + core_square))
        ).astype(jnp.bfloat16)
        partner_values = partner_data[:rhs_count].astype(jnp.bfloat16)
        return jnp.einsum(
            "lisj,rlsj->rli", kernel, partner_values, preferred_element_type=jnp.float32
        )

    blocks_out = lax.map(near_block, jnp.arange(leaf_count // 8, dtype=jnp.int32))
    return jnp.transpose(blocks_out, (1, 0, 2, 3)).reshape(rhs_count, leaf_count * leaf_size)


def local(
    densities,
    points,
    weights,
    near_offsets,
    leaf_basis,
    transfer,
    send_lists,
    relay_refs,
    leaf_coupling,
    coarse_refs,
    coarse_coupling,
):
    near_part = near_field(densities, points, weights, near_offsets)
    rhs_count = densities.shape[0]
    leaf_count, basis_rank, leaf_size = leaf_basis.shape
    values = densities.reshape(rhs_count, leaf_count, leaf_size)
    coeff0 = jnp.einsum(
        "lkm,rlm->lrk", leaf_basis, values, preferred_element_type=jnp.float32
    ).astype(jnp.bfloat16)
    capacity = send_lists.shape[2]
    outgoing = jnp.take(coeff0, send_lists[0], axis=0)
    pieces = []
    for window_index in range(2 * WINDOW + 1):
        offset = window_index - WINDOW
        if offset == 0:
            pieces.append(outgoing[WINDOW])
        else:
            pieces.append(from_behind(outgoing[2 * WINDOW - window_index], ("gx", "gy"), -offset))
    received = jnp.stack(pieces, axis=0)
    received = received.reshape((2 * WINDOW + 1) * capacity, rhs_count, basis_rank)
    picked = jnp.take(received, relay_refs, axis=0)
    local0 = jnp.einsum("lsab,lsrb->lra", leaf_coupling, picked, preferred_element_type=jnp.float32)
    groups = leaf_count // 8
    transfer_groups = transfer.reshape(groups, 8, basis_rank, basis_rank)
    coeff1 = jnp.einsum(
        "qcab,qcra->qrb",
        transfer_groups,
        coeff0.reshape(groups, 8, rhs_count, basis_rank),
        preferred_element_type=jnp.float32,
    ).astype(jnp.bfloat16)
    everyone = lax.all_gather(coeff1, ("gx", "gy"), axis=0, tiled=True)
    coarse_picked = jnp.take(everyone, coarse_refs, axis=0)
    local1 = jnp.einsum(
        "qsab,qsrb->qra", coarse_coupling, coarse_picked, preferred_element_type=jnp.float32
    ).astype(jnp.bfloat16)
    downward = jnp.einsum(
        "qcab,qrb->qcra", transfer_groups, local1, preferred_element_type=jnp.float32
    ).reshape(leaf_count, rhs_count, basis_rank)
    leaf_field = (local0 + downward).astype(jnp.bfloat16)
    far_field = jnp.einsum(
        "lkm,lrk->rlm", leaf_basis, leaf_field, preferred_element_type=jnp.float32
    ).reshape(rhs_count, leaf_count * leaf_size)
    return far_field + near_part


def solution(mesh):
    in_specs = (
        P(None, ("gx", "gy")),
        P(None, ("gx", "gy")),
        P(("gx", "gy")),
        P(("gx", "gy"), None),
        P(("gx", "gy"), None, None),
        P(("gx", "gy"), None, None),
        P(("gx", "gy"), None, None),
        P(("gx", "gy"), None),
        P(("gx", "gy"), None, None, None),
        P(("gx", "gy"), None),
        P(("gx", "gy"), None, None, None),
    )
    out_specs = P(None, ("gx", "gy"))
    return jax.shard_map(local, mesh=mesh, in_specs=in_specs, out_specs=out_specs, check_vma=False)
```

profile of v0, /device:TPU:0, one launch (start us, length us, event | category | flops | bytes accessed | tf_op | source)
XLA Modules:
  0.0 197.4 jit_solution(12557109783753308516)
XLA Ops:
  1.8 1.5 convolution_convert_fusion
  3.3 2.0 %gather_fusion.1 = bf16[272,16,64]{2,1,0:T(8,128)(2,1)S(1)} fusion(bf16[32,16,64]{2,1,0:T(8,128)(2,1)S(1)} %convolution_convert_fusion, s32[1024]{0:T(1024)S(1)} %pad_clamp_fusion.2), kind=kCustom, calls=%fused_computation.1 | custom fusion | bytes 1115200 | tf_op jit(solution)/shard_map/jit(_take)/gather | solution.py:83
  6.7 5.6 %collective-permute-start = (bf16[16,16,64]{2,1,0:T(8,128)(2,1)S(1)}, bf16[16,16,64]{2,1,0:T(8,128)(2,1)}, u32[]{:S(2)}, u32[]{:S(2)}) collective-permute-start(bf16[16,16,64]{2,1,0:T(8,128)(2,1)S(1)} %get-tuple-element.91), channel_id=1, source_target_pairs={{0,8},{1,9},{2,10},{3,11},{4,12},{5,13},{6,14},{7,15},{8,16},{9,17... | collective-permute-start | bytes 98312 | tf_op jit(solution)/shard_map/ppermute | solution.py:19
  12.3 5.3 %collective-permute-start.1 = (bf16[16,16,64]{2,1,0:T(8,128)(2,1)}, bf16[16,16,64]{2,1,0:T(8,128)(2,1)}, u32[]{:S(2)}, u32[]{:S(2)}) collective-permute-start(bf16[16,16,64]{2,1,0:T(8,128)(2,1)} %get-tuple-element.90), channel_id=1, source_target_pairs={{0,7},{1,8},{2,9},{3,10},{4,11},{5,12},{6,13},{7,14},{8,15},{9,16}... | collective-permute-start | bytes 98312 | tf_op jit(solution)/shard_map/ppermute | solution.py:19
  17.5 3.3 %collective-permute-start.2 = (bf16[16,16,64]{2,1,0:T(8,128)(2,1)}, bf16[16,16,64]{2,1,0:T(8,128)(2,1)}, u32[]{:S(2)}, u32[]{:S(2)}) collective-permute-start(bf16[16,16,64]{2,1,0:T(8,128)(2,1)} %get-tuple-element.89), channel_id=1, source_target_pairs={{0,6},{1,7},{2,8},{3,9},{4,10},{5,11},{6,12},{7,13},{8,14},{9,15},... | collective-permute-start | bytes 98312 | tf_op jit(solution)/shard_map/ppermute | solution.py:19
  20.8 2.7 %collective-permute-start.3 = (bf16[16,16,64]{2,1,0:T(8,128)(2,1)}, bf16[16,16,64]{2,1,0:T(8,128)(2,1)}, u32[]{:S(2)}, u32[]{:S(2)}) collective-permute-start(bf16[16,16,64]{2,1,0:T(8,128)(2,1)} %get-tuple-element.88), channel_id=1, source_target_pairs={{0,5},{1,6},{2,7},{3,8},{4,9},{5,10},{6,11},{7,12},{8,13},{9,14},{... | collective-permute-start | bytes 98312 | tf_op jit(solution)/shard_map/ppermute | solution.py:19
  23.5 5.4 %collective-permute-start.4 = (bf16[16,16,64]{2,1,0:T(8,128)(2,1)}, bf16[16,16,64]{2,1,0:T(8,128)(2,1)}, u32[]{:S(2)}, u32[]{:S(2)}) collective-permute-start(bf16[16,16,64]{2,1,0:T(8,128)(2,1)} %get-tuple-element.87), channel_id=1, source_target_pairs={{0,4},{1,5},{2,6},{3,7},{4,8},{5,9},{6,10},{7,11},{8,12},{9,13},{1... | collective-permute-start | bytes 98312 | tf_op jit(solution)/shard_map/ppermute | solution.py:19
  31.0 38.6 %all_gather.3 = bf16[128,16,64]{2,1,0:T(8,128)(2,1)S(1)} all-gather(bf16[4,16,64]{2,1,0:T(8,128)(2,1)S(1)} %fusion.18), channel_id=1, replica_groups=mesh['gx'=4,'gy'=8] {'gx','gy'}, dimensions={0}, use_global_device_ids=true | all-gather | bytes 270336 | tf_op jit(solution)/shard_map/all_gather | solution.py:103
  69.8 1.5 gather_fusion.3
  72.0 2.9 %fusion.21 = f32[4,16,8,64]{3,1,2,0:T(8,128)} fusion(bf16[4,8,64,64]{3,2,1,0:T(8,128)(2,1)S(1)} %bitcast.194, bf16[4,32,64,64]{3,2,1,0:T(8,128)(2,1)S(1)} %copy-done, bf16[4,32,16,64]{3,2,1,0:T(8,128)(2,1)} %bitcast.195, pred[4,32]{1,0:T(4,128)(4,1)} %compare_and_fusion.3), kind=kOutput, calls=%fused_computation.37 | convolution fusion | flops 21106688 | bytes 1704064 | tf_op jit(solution)/shard_map/qcab,qrb->qcra/dot_general | solution.py:108
  76.9 3.6 %collective-permute-start.5 = (bf16[16,16,64]{2,1,0:T(8,128)(2,1)}, bf16[16,16,64]{2,1,0:T(8,128)(2,1)S(1)}, u32[]{:S(2)}, u32[]{:S(2)}) collective-permute-start(bf16[16,16,64]{2,1,0:T(8,128)(2,1)} %get-tuple-element.86), channel_id=1, source_target_pairs={{0,3},{1,4},{2,5},{3,6},{4,7},{5,8},{6,9},{7,10},{8,11},{9,12},{10... | collective-permute-start | bytes 98312 | tf_op jit(solution)/shard_map/ppermute | solution.py:19
  81.4 1.3 collective-permute-start.6
  83.6 2.6 %collective-permute-start.7 = (bf16[16,16,64]{2,1,0:T(8,128)(2,1)}, bf16[16,16,64]{2,1,0:T(8,128)(2,1)S(1)}, u32[]{:S(2)}, u32[]{:S(2)}) collective-permute-start(bf16[16,16,64]{2,1,0:T(8,128)(2,1)} %get-tuple-element.84), channel_id=1, source_target_pairs={{0,1},{1,2},{2,3},{3,4},{4,5},{5,6},{6,7},{7,8},{8,9},{9,10},{10,1... | collective-permute-start | bytes 98312 | tf_op jit(solution)/shard_map/ppermute | solution.py:19
  87.0 2.5 %collective-permute-start.16 = (bf16[20,1024]{1,0:T(8,128)(2,1)}, bf16[20,1024]{1,0:T(8,128)(2,1)}, u32[]{:S(2)}, u32[]{:S(2)}) collective-permute-start(bf16[20,1024]{1,0:T(8,128)(2,1)} %slice.154), channel_id=1, source_target_pairs={{0,1},{1,2},{2,3},{3,4},{4,5},{5,6},{6,7},{7,8},{8,9},{9,10},{10,1... | collective-permute-start | bytes 122888 | tf_op jit(solution)/shard_map/ppermute | solution.py:19
  90.4 1.3 collective-permute-start.17
  92.7 1.9 slice_bitcast_fusion
  94.6 1.3 collective-permute-start.8
  97.1 1.3 collective-permute-start.9
  98.4 1.3 collective-permute-start.10
  99.7 1.3 collective-permute-start.11
  101.0 1.5 convert_element_type.28
  102.5 1.3 collective-permute-start.12
  105.0 1.3 collective-permute-start.13
  106.3 1.3 collective-permute-start.14
  107.6 4.3 %collective-permute-done.11 = bf16[16,16,64]{2,1,0:T(8,128)(2,1)S(1)} collective-permute-done((bf16[16,16,64]{2,1,0:T(8,128)(2,1)}, bf16[16,16,64]{2,1,0:T(8,128)(2,1)S(1)}, u32[]{:S(2)}, u32[]{:S(2)}) %collective-permute-start.11) | collective-permute-done | bytes 32800 | tf_op jit(solution)/shard_map/ppermute | solution.py:19
  111.9 1.3 collective-permute-start.15
  113.2 4.2 %collective-permute-done.13 = bf16[16,16,64]{2,1,0:T(8,128)(2,1)S(1)} collective-permute-done((bf16[16,16,64]{2,1,0:T(8,128)(2,1)}, bf16[16,16,64]{2,1,0:T(8,128)(2,1)S(1)}, u32[]{:S(2)}, u32[]{:S(2)}) %collective-permute-start.13) | collective-permute-done | bytes 32800 | tf_op jit(solution)/shard_map/ppermute | solution.py:19
  117.4 1.8 collective-permute-done.14
  119.2 2.6 %collective-permute-done.15 = bf16[16,16,64]{2,1,0:T(8,128)(2,1)S(1)} collective-permute-done((bf16[16,16,64]{2,1,0:T(8,128)(2,1)}, bf16[16,16,64]{2,1,0:T(8,128)(2,1)S(1)}, u32[]{:S(2)}, u32[]{:S(2)}) %collective-permute-start.15) | collective-permute-done | bytes 32800 | tf_op jit(solution)/shard_map/ppermute | solution.py:19
  121.8 8.5 %gather_fusion.2 = bf16[1024,16,64]{2,1,0:T(8,128)(2,1)} fusion(bf16[272,16,64]{2,1,0:T(8,128)(2,1)S(1)} %bitcast.188, s32[1024]{0:T(1024)} %broadcast_clamp_fusion), kind=kCustom, calls=%fused_computation.2 | custom fusion | bytes 4198400 | tf_op jit(solution)/shard_map/jit(_take)/gather | solution.py:93
  130.3 10.4 %convolution_bitcast_fusion = f32[32,2,8,128]{3,2,1,0:T(8,128)} fusion(bf16[32,64,128]{2,1,0:T(8,128)(2,1)} %param.17, f32[32,16,64]{2,1,0:T(8,128)} %bitcast.199, bf16[32,32,64,64]{3,2,1,0:T(8,128)(2,1)} %param.21, bf16[32,32,16,64]{3,2,1,0:T(8,128)(2,1)} %bitcast.191, pred[32,32]{1,0:T(8,128)(4,1)} %compare_and_fusion.1), kind=kOutput, calls=%fused_computation.26 | convolution fusion | flops 143720448 | bytes 11404288 | tf_op jit(solution)/shard_map/lkm,lrk->rlm/dot_general | solution.py:112
  140.7 0.9 pad_maximum_fusion
  141.8 1.0 copy.59
  142.8 51.7 %while.10 = (s32[]{:T(128)}, f32[4,16,8,128]{3,1,2,0:T(8,128)}, s32[4]{0:T(128)S(1)}, s32[32,13]{1,0:T(8,128)}, f32[20,48,128]{2,0,1:T(8,128)}, /*index=5*/f32[3...) while((s32[]{:T(128)}, f32[4,16,8,128]{3,1,2,0:T(8,128)}, ...), condition=%wide.region_1.2_spmd, body=%wide.region_0.1_spmd.sunk | while | flops 75241080 | bytes 10120579 | solution.py:58
  144.9 1.7 gather_fusion
  146.8 1.1 copy-done.1
  148.7 7.0 %fusion.48 = f32[4,16,8,128]{3,1,2,0:T(8,128)} fusion(f32[4,16,8,128]{3,1,2,0:T(8,128)} %get-tuple-element.168, s32[]{:T(128)} %get-tuple-element.167, f32[8,13,128]{2,1,0:T(8,128)S(1)} %get-tuple-element.146, f32[8,128]{1,0:T(8,128)S(1)} %get-tuple-element.147, f32[8,13,128]{2,1,0:T(8,128)S(1)} %get-tuple-element.148, ...), kind=kOutput, calls=%fused_computation.8.clone.1 | convolution fusion | flops 74973184 | bytes 717312 | tf_op jit(solution)/shard_map/while/body/eval_jaxpr/lisj,rlsj->rli/dot_general | solution.py:54
  157.8 1.7 gather_fusion
  159.7 1.1 copy-done.1
  161.7 7.0 %fusion.48 = f32[4,16,8,128]{3,1,2,0:T(8,128)} fusion(f32[4,16,8,128]{3,1,2,0:T(8,128)} %get-tuple-element.168, s32[]{:T(128)} %get-tuple-element.167, f32[8,13,128]{2,1,0:T(8,128)S(1)} %get-tuple-element.146, f32[8,128]{1,0:T(8,128)S(1)} %get-tuple-element.147, f32[8,13,128]{2,1,0:T(8,128)S(1)} %get-tuple-element.148, ...), kind=kOutput, calls=%fused_computation.8.clone.1 | convolution fusion | flops 74973184 | bytes 717312 | tf_op jit(solution)/shard_map/while/body/eval_jaxpr/lisj,rlsj->rli/dot_general | solution.py:54
  170.8 1.7 gather_fusion
  172.7 1.1 copy-done.1
  174.6 7.0 %fusion.48 = f32[4,16,8,128]{3,1,2,0:T(8,128)} fusion(f32[4,16,8,128]{3,1,2,0:T(8,128)} %get-tuple-element.168, s32[]{:T(128)} %get-tuple-element.167, f32[8,13,128]{2,1,0:T(8,128)S(1)} %get-tuple-element.146, f32[8,128]{1,0:T(8,128)S(1)} %get-tuple-element.147, f32[8,13,128]{2,1,0:T(8,128)S(1)} %get-tuple-element.148, ...), kind=kOutput, calls=%fused_computation.8.clone.1 | convolution fusion | flops 74973184 | bytes 717312 | tf_op jit(solution)/shard_map/while/body/eval_jaxpr/lisj,rlsj->rli/dot_general | solution.py:54
  183.7 1.7 gather_fusion
  185.6 1.1 copy-done.1
  187.5 7.0 %fusion.48 = f32[4,16,8,128]{3,1,2,0:T(8,128)} fusion(f32[4,16,8,128]{3,1,2,0:T(8,128)} %get-tuple-element.168, s32[]{:T(128)} %get-tuple-element.167, f32[8,13,128]{2,1,0:T(8,128)S(1)} %get-tuple-element.146, f32[8,128]{1,0:T(8,128)S(1)} %get-tuple-element.147, f32[8,13,128]{2,1,0:T(8,128)S(1)} %get-tuple-element.148, ...), kind=kOutput, calls=%fused_computation.8.clone.1 | convolution fusion | flops 74973184 | bytes 717312 | tf_op jit(solution)/shard_map/while/body/eval_jaxpr/lisj,rlsj->rli/dot_general | solution.py:54
  194.5 1.0 copy.60
  195.5 1.8 bitcast_add_fusion
  (123 shorter events, 24.9 us)
Async XLA Ops:
  0.0 72.0 %copy-start = (bf16[4,32,64,64]{3,2,1,0:T(8,128)(2,1)S(1)}, bf16[4,32,64,64]{3,2,1,0:T(8,128)(2,1)}, u32[]{:S(2)}) copy-start(bf16[4,32,64,64]{3,2,1,0:T(8,128)(2,1)} %param.23) | copy-start | bytes 3145732
  5.3 23.6 %copy-start.12 = (s32[4,32]{1,0:T(4,128)S(1)}, s32[4,32]{1,0:T(4,128)}, u32[]{:S(2)}) copy-start(s32[4,32]{1,0:T(4,128)} %param.22) | copy-start | bytes 1540
  5.3 24.2 %copy-start.8 = (s32[32,32]{1,0:T(8,128)S(1)}, s32[32,32]{1,0:T(8,128)}, u32[]{:S(2)}) copy-start(s32[32,32]{1,0:T(8,128)} %param.20) | copy-start | bytes 12292
  5.8 25.1 %copy-start.2 = (bf16[17,16,16,64]{3,2,1,0:T(8,128)(2,1)}, bf16[17,16,16,64]{3,2,1,0:T(8,128)(2,1)S(1)}, u32[]{:S(2)}) copy-start(bf16[17,16,16,64]{3,2,1,0:T(8,128)(2,1)S(1)} %broadcast_select_fusion) | copy-start | bytes 1671172
  5.9 24.8 %copy-start.5 = (bf16[16,4096]{1,0:T(8,128)(2,1)S(1)}, bf16[16,4096]{1,0:T(8,128)(2,1)}, u32[]{:S(2)}) copy-start(bf16[16,4096]{1,0:T(8,128)(2,1)} %param.13) | copy-start | bytes 393220
  5.9 24.9 %copy-start.3 = (bf16[32,64,64]{2,1,0:T(8,128)(2,1)S(1)}, bf16[32,64,64]{2,1,0:T(8,128)(2,1)}, u32[]{:S(2)}) copy-start(bf16[32,64,64]{2,1,0:T(8,128)(2,1)} %param.18) | copy-start | bytes 786436
  5.9 63.8 %copy-start.11 = (s32[32,13]{0,1:T(8,128)S(1)}, s32[32,13]{0,1:T(8,128)}, u32[]{:S(2)}) copy-start(s32[32,13]{0,1:T(8,128)} %param.16) | copy-start | bytes 4996
  6.7 70.2 %collective-permute-start = (bf16[16,16,64]{2,1,0:T(8,128)(2,1)S(1)}, bf16[16,16,64]{2,1,0:T(8,128)(2,1)}, u32[]{:S(2)}, u32[]{:S(2)}) collective-permute-start(bf16[16,16,64]{2,1,0:T(8,128)(2,1)S(1)} %get-tuple-element.91), channel_id=1, source_target_pairs={{0,8},{1,9},{2,10},{3,11},{4,12},{5,13},{6,14},{7,15},{8,16},{9,17... | collective-permute-start | bytes 98312 | tf_op jit(solution)/shard_map/ppermute | solution.py:19
  12.3 69.1 %collective-permute-start.1 = (bf16[16,16,64]{2,1,0:T(8,128)(2,1)}, bf16[16,16,64]{2,1,0:T(8,128)(2,1)}, u32[]{:S(2)}, u32[]{:S(2)}) collective-permute-start(bf16[16,16,64]{2,1,0:T(8,128)(2,1)} %get-tuple-element.90), channel_id=1, source_target_pairs={{0,7},{1,8},{2,9},{3,10},{4,11},{5,12},{6,13},{7,14},{8,15},{9,16}... | collective-permute-start | bytes 98312 | tf_op jit(solution)/shard_map/ppermute | solution.py:19
  17.5 66.0 %collective-permute-start.2 = (bf16[16,16,64]{2,1,0:T(8,128)(2,1)}, bf16[16,16,64]{2,1,0:T(8,128)(2,1)}, u32[]{:S(2)}, u32[]{:S(2)}) collective-permute-start(bf16[16,16,64]{2,1,0:T(8,128)(2,1)} %get-tuple-element.89), channel_id=1, source_target_pairs={{0,6},{1,7},{2,8},{3,9},{4,10},{5,11},{6,12},{7,13},{8,14},{9,15},... | collective-permute-start | bytes 98312 | tf_op jit(solution)/shard_map/ppermute | solution.py:19
  20.8 66.2 %collective-permute-start.3 = (bf16[16,16,64]{2,1,0:T(8,128)(2,1)}, bf16[16,16,64]{2,1,0:T(8,128)(2,1)}, u32[]{:S(2)}, u32[]{:S(2)}) collective-permute-start(bf16[16,16,64]{2,1,0:T(8,128)(2,1)} %get-tuple-element.88), channel_id=1, source_target_pairs={{0,5},{1,6},{2,7},{3,8},{4,9},{5,10},{6,11},{7,12},{8,13},{9,14},{... | collective-permute-start | bytes 98312 | tf_op jit(solution)/shard_map/ppermute | solution.py:19
  23.5 66.9 %collective-permute-start.4 = (bf16[16,16,64]{2,1,0:T(8,128)(2,1)}, bf16[16,16,64]{2,1,0:T(8,128)(2,1)}, u32[]{:S(2)}, u32[]{:S(2)}) collective-permute-start(bf16[16,16,64]{2,1,0:T(8,128)(2,1)} %get-tuple-element.87), channel_id=1, source_target_pairs={{0,4},{1,5},{2,6},{3,7},{4,8},{5,9},{6,10},{7,11},{8,12},{9,13},{1... | collective-permute-start | bytes 98312 | tf_op jit(solution)/shard_map/ppermute | solution.py:19
  72.0 2.9 %copy-start.4 = (f32[3,4096]{1,0:T(4,128)S(1)}, f32[3,4096]{1,0:T(4,128)}, u32[]{:S(2)}) copy-start(f32[3,4096]{1,0:T(4,128)} %param.14) | copy-start | bytes 147460
  72.0 2.9 %copy-start.7 = (f32[4096]{0:T(1024)S(1)}, f32[4096]{0:T(1024)}, u32[]{:S(2)}) copy-start(f32[4096]{0:T(1024)} %param.15) | copy-start | bytes 49156
  72.0 3.6 %copy-start.9 = (s32[32,32]{1,0:T(8,128)S(1)}, s32[32,32]{1,0:T(8,128)}, u32[]{:S(2)}) copy-start(s32[32,32]{1,0:T(8,128)} %compare_select_fusion.1) | copy-start | bytes 12292
  76.9 19.0 %copy-start.10 = (s32[1024]{0:T(1024)S(1)}, s32[1024]{0:T(1024)}, u32[]{:S(2)}) copy-start(s32[1024]{0:T(1024)} %reshape.117) | copy-start | bytes 12292
  76.9 15.7 %collective-permute-start.5 = (bf16[16,16,64]{2,1,0:T(8,128)(2,1)}, bf16[16,16,64]{2,1,0:T(8,128)(2,1)S(1)}, u32[]{:S(2)}, u32[]{:S(2)}) collective-permute-start(bf16[16,16,64]{2,1,0:T(8,128)(2,1)} %get-tuple-element.86), channel_id=1, source_target_pairs={{0,3},{1,4},{2,5},{3,6},{4,7},{5,8},{6,9},{7,10},{8,11},{9,12},{10... | collective-permute-start | bytes 98312 | tf_op jit(solution)/shard_map/ppermute | solution.py:19
  81.4 11.3 %collective-permute-start.6 = (bf16[16,16,64]{2,1,0:T(8,128)(2,1)}, bf16[16,16,64]{2,1,0:T(8,128)(2,1)S(1)}, u32[]{:S(2)}, u32[]{:S(2)}) collective-permute-start(bf16[16,16,64]{2,1,0:T(8,128)(2,1)} %get-tuple-element.85), channel_id=1, source_target_pairs={{0,2},{1,3},{2,4},{3,5},{4,6},{5,7},{6,8},{7,9},{8,10},{9,11},{10,... | collective-permute-start | bytes 98312 | tf_op jit(solution)/shard_map/ppermute | solution.py:19
  83.6 9.1 %collective-permute-start.7 = (bf16[16,16,64]{2,1,0:T(8,128)(2,1)}, bf16[16,16,64]{2,1,0:T(8,128)(2,1)S(1)}, u32[]{:S(2)}, u32[]{:S(2)}) collective-permute-start(bf16[16,16,64]{2,1,0:T(8,128)(2,1)} %get-tuple-element.84), channel_id=1, source_target_pairs={{0,1},{1,2},{2,3},{3,4},{4,5},{5,6},{6,7},{7,8},{8,9},{9,10},{10,1... | collective-permute-start | bytes 98312 | tf_op jit(solution)/shard_map/ppermute | solution.py:19
  87.0 12.7 %collective-permute-start.16 = (bf16[20,1024]{1,0:T(8,128)(2,1)}, bf16[20,1024]{1,0:T(8,128)(2,1)}, u32[]{:S(2)}, u32[]{:S(2)}) collective-permute-start(bf16[20,1024]{1,0:T(8,128)(2,1)} %slice.154), channel_id=1, source_target_pairs={{0,1},{1,2},{2,3},{3,4},{4,5},{5,6},{6,7},{7,8},{8,9},{9,10},{10,1... | collective-permute-start | bytes 122888 | tf_op jit(solution)/shard_map/ppermute | solution.py:19
  90.4 50.2 %collective-permute-start.17 = (f32[20,1024]{1,0:T(8,128)}, f32[20,1024]{1,0:T(8,128)}, u32[]{:S(2)}, u32[]{:S(2)}) collective-permute-start(f32[20,1024]{1,0:T(8,128)} %pad_maximum_fusion.2), channel_id=1, source_target_pairs={{1,0},{2,1},{3,2},{4,3},{5,4},{6,5},{7,6},{8,7},{9,8},{10,9},{11,1... | collective-permute-start | bytes 245768 | tf_op jit(solution)/shard_map/ppermute | solution.py:19
  94.6 7.9 %collective-permute-start.8 = (bf16[16,16,64]{2,1,0:T(8,128)(2,1)}, bf16[16,16,64]{2,1,0:T(8,128)(2,1)}, u32[]{:S(2)}, u32[]{:S(2)}) collective-permute-start(bf16[16,16,64]{2,1,0:T(8,128)(2,1)} %get-tuple-element.82), channel_id=1, source_target_pairs={{1,0},{2,1},{3,2},{4,3},{5,4},{6,5},{7,6},{8,7},{9,8},{10,9},{11,1... | collective-permute-start | bytes 98312 | tf_op jit(solution)/shard_map/ppermute | solution.py:19
  97.1 7.8 %collective-permute-start.9 = (bf16[16,16,64]{2,1,0:T(8,128)(2,1)}, bf16[16,16,64]{2,1,0:T(8,128)(2,1)S(1)}, u32[]{:S(2)}, u32[]{:S(2)}) collective-permute-start(bf16[16,16,64]{2,1,0:T(8,128)(2,1)} %get-tuple-element.81), channel_id=1, source_target_pairs={{2,0},{3,1},{4,2},{5,3},{6,4},{7,5},{8,6},{9,7},{10,8},{11,9},{12,... | collective-permute-start | bytes 98312 | tf_op jit(solution)/shard_map/ppermute | solution.py:19
  98.4 7.9 %collective-permute-start.10 = (bf16[16,16,64]{2,1,0:T(8,128)(2,1)}, bf16[16,16,64]{2,1,0:T(8,128)(2,1)S(1)}, u32[]{:S(2)}, u32[]{:S(2)}) collective-permute-start(bf16[16,16,64]{2,1,0:T(8,128)(2,1)} %get-tuple-element.80), channel_id=1, source_target_pairs={{3,0},{4,1},{5,2},{6,3},{7,4},{8,5},{9,6},{10,7},{11,8},{12,9},{13... | collective-permute-start | bytes 98312 | tf_op jit(solution)/shard_map/ppermute | solution.py:19
  99.7 12.2 %collective-permute-start.11 = (bf16[16,16,64]{2,1,0:T(8,128)(2,1)}, bf16[16,16,64]{2,1,0:T(8,128)(2,1)S(1)}, u32[]{:S(2)}, u32[]{:S(2)}) collective-permute-start(bf16[16,16,64]{2,1,0:T(8,128)(2,1)} %get-tuple-element.79), channel_id=1, source_target_pairs={{4,0},{5,1},{6,2},{7,3},{8,4},{9,5},{10,6},{11,7},{12,8},{13,9},{1... | collective-permute-start | bytes 98312 | tf_op jit(solution)/shard_map/ppermute | solution.py:19
  102.5 10.7 %collective-permute-start.12 = (bf16[16,16,64]{2,1,0:T(8,128)(2,1)}, bf16[16,16,64]{2,1,0:T(8,128)(2,1)S(1)}, u32[]{:S(2)}, u32[]{:S(2)}) collective-permute-start(bf16[16,16,64]{2,1,0:T(8,128)(2,1)} %get-tuple-element.78), channel_id=1, source_target_pairs={{5,0},{6,1},{7,2},{8,3},{9,4},{10,5},{11,6},{12,7},{13,8},{14,9},{... | collective-permute-start | bytes 98312 | tf_op jit(solution)/shard_map/ppermute | solution.py:19
  105.0 12.4 %collective-permute-start.13 = (bf16[16,16,64]{2,1,0:T(8,128)(2,1)}, bf16[16,16,64]{2,1,0:T(8,128)(2,1)S(1)}, u32[]{:S(2)}, u32[]{:S(2)}) collective-permute-start(bf16[16,16,64]{2,1,0:T(8,128)(2,1)} %get-tuple-element.77), channel_id=1, source_target_pairs={{6,0},{7,1},{8,2},{9,3},{10,4},{11,5},{12,6},{13,7},{14,8},{15,9},... | collective-permute-start | bytes 98312 | tf_op jit(solution)/shard_map/ppermute | solution.py:19
  106.3 12.9 %collective-permute-start.14 = (bf16[16,16,64]{2,1,0:T(8,128)(2,1)}, bf16[16,16,64]{2,1,0:T(8,128)(2,1)S(1)}, u32[]{:S(2)}, u32[]{:S(2)}) collective-permute-start(bf16[16,16,64]{2,1,0:T(8,128)(2,1)} %get-tuple-element.76), channel_id=1, source_target_pairs={{7,0},{8,1},{9,2},{10,3},{11,4},{12,5},{13,6},{14,7},{15,8},{16,9}... | collective-permute-start | bytes 98312 | tf_op jit(solution)/shard_map/ppermute | solution.py:19
  111.9 9.9 %collective-permute-start.15 = (bf16[16,16,64]{2,1,0:T(8,128)(2,1)}, bf16[16,16,64]{2,1,0:T(8,128)(2,1)S(1)}, u32[]{:S(2)}, u32[]{:S(2)}) collective-permute-start(bf16[16,16,64]{2,1,0:T(8,128)(2,1)} %get-tuple-element.75), channel_id=1, source_target_pairs={{8,0},{9,1},{10,2},{11,3},{12,4},{13,5},{14,6},{15,7},{16,8},{17,9... | collective-permute-start | bytes 98312 | tf_op jit(solution)/shard_map/ppermute | solution.py:19
  130.3 10.4 %copy-start.6 = (f32[20,1024]{1,0:T(8,128)S(1)}, f32[20,1024]{1,0:T(8,128)}, u32[]{:S(2)}) copy-start(f32[20,1024]{1,0:T(8,128)} %convert_element_type.28) | copy-start | bytes 245764
  146.8 1.1 copy-start.1
  159.7 1.1 copy-start.1
  172.7 1.1 copy-start.1
  185.6 1.1 copy-start.1
where the time goes:
time: 201 us; the launch traced here: 197 us
  starting transfers between devices  43.9 us (22%)
  matrix products  42.8 us (21%)
  local copies, waits for them, and re-layouts  42 us (21%)
  blocking collectives  38.6 us (19%)
  other arithmetic  13.5 us (7%)
  waiting for transfers between devices  13.2 us (7%)
  loops' own time  2.91 us (1%)
    ppermute x18, starting transfers between devices, from_behind(): return lax.ppermute(shard, axis, pairs)  43.9 us
    all_gather x1, blocking collectives, local(): everyone = lax.all_gather(coeff1, ('gx', 'gy'), axis=0, tiled=True)  38.6 us
    dot_general x4, matrix products, near_block(): jnp.einsum('lisj,rlsj->rli', kernel, partner_values, preferred_element_ty...  27.8 us
    ppermute x18, waiting for transfers between devices, from_behind(): return lax.ppermute(shard, axis, pairs)  13.2 us
    dot_general x1, matrix products, local(): jnp.einsum('lkm,lrk->rlm', leaf_basis, leaf_field, preferred_element_type...  10.4 us
    gather x1, local copies, waits for them, and re-layouts, local(): picked = jnp.take(received, relay_refs, axis=0)  8.46 us
    gather x4, local copies, waits for them, and re-layouts, near_block(): partner_data = jnp.take(extended, partner_rows, axis=1)  6.81 us
    unnamed x42, local copies, waits for them, and re-layouts  6.1 us
  transfers between devices with their start and end apart: 18, of which 5 were waited for; matrix products, arithmetic and copies ran while one was open for 19% of the time, Pallas kernels for 0%

commit v1 on v0

v1 whole, which is shorter than its diff:
```python
import functools
import math

import jax
import jax.numpy as jnp
from jax import lax
from jax.experimental import pallas as pl
from jax.experimental.pallas import tpu as pltpu
from jax.sharding import PartitionSpec as P

REACH = 8
WINDOW = 8
CHILDREN = 8
WINDOWS = 2 * WINDOW + 1

core_square = 0.0004
four_pi = 4.0 * math.pi

MESH = pl.DeviceIdType.MESH
ROWS_BY_ROWS = (((1,), (1,)), ((), ()))
PLAIN = (((1,), (0,)), ((), ()))


def dot(left, right, dims):
    return lax.dot_general(left, right, dims, preferred_element_type=jnp.float32)


def split(values):
    first = values.astype(jnp.bfloat16).astype(jnp.float32)
    rest = values - first
    second = rest.astype(jnp.bfloat16).astype(jnp.float32)
    return first, second, rest - second


def features(pack):
    row = lax.broadcasted_iota(jnp.int32, pack.shape, 0)
    shifted = pack - 0.5
    squares = shifted * shifted
    norm = squares[0:1] + squares[1:2] + squares[2:3]
    root = four_pi / pack[3:4]
    scale = root * root
    left = jnp.where(row < 3, shifted, jnp.where(row == 3, norm, jnp.where(row == 4, 1.0, 0.0)))
    right = scale * jnp.where(
        row < 3,
        -2.0 * shifted,
        jnp.where(row == 3, 1.0, jnp.where(row == 4, norm + core_square, 0.0)),
    )
    a1, a2, a3 = split(left)
    b1, b2, b3 = split(right)
    return (
        jnp.concatenate([a1, a1, a2, a1, a3, a2], axis=0),
        jnp.concatenate([b1, b2, b1, b3, b1, b2], axis=0),
    )


def exchange_kernel(
    sizes,
    offsets_ref,
    lists_ref,
    dens_ref,
    pack_ref,
    basis_ref,
    transfer_ref,
    near_ref,
    listed_ref,
    coarse_ref,
    row_feat,
    col_feat,
    values,
    coeff,
    outgoing,
    halo_dens,
    halo_pack,
    halo_send,
    halo_recv,
    list_send,
    list_recv,
    coarse_send,
    coarse_recv,
):
    n_gx, n_gy = sizes
    total = n_gx * n_gy
    me = lax.axis_index("gx") * n_gy + lax.axis_index("gy")
    leaf_count, rank, leaf_size = basis_ref.shape
    slots = offsets_ref.shape[1]
    groups = leaf_count // CHILDREN
    half_slots = lists_ref.shape[1] // 2
    rim = REACH * leaf_size
    columns = leaf_count * leaf_size

    def place(index):
        return (index // n_gy, index % n_gy)

    barrier = pltpu.get_barrier_semaphore()

    def greet(step, carry):
        other = (me + step) % total
        pl.semaphore_signal(barrier, inc=1, device_id=place(other), device_id_type=MESH)
        return carry

    lax.fori_loop(1, total, greet, 0)

    low = lax.broadcasted_iota(jnp.int32, (dens_ref.shape[0], 2 * rank), 1) < rank

    def upward(pair, carry):
        parents = []
        for g in range(2):
            parent = None
            for child in range(CHILDREN):
                leaf = (pair * 2 + g) * CHILDREN + child
                start = pl.multiple_of(leaf * leaf_size, leaf_size)
                basis = basis_ref[leaf]
                doubled = jnp.concatenate([basis, basis], axis=0)
                both = dot(dens_ref[:, pl.ds(start, leaf_size)], doubled, ROWS_BY_ROWS)
                both = both.astype(jnp.bfloat16)
                coeff[leaf] = both
                term = dot(both[:, :rank], transfer_ref[leaf], PLAIN)
                parent = term if parent is None else parent + term
            parents.append(parent)
        coarse_ref[me, pair] = jnp.concatenate(parents, axis=1).astype(jnp.bfloat16)
        return carry

    lax.fori_loop(0, groups // 2, upward, 0)

    def gather(window, carry):
        for slot in range(half_slots):
            first = coeff[lists_ref[window, slot]]
            second = coeff[lists_ref[window, slot + half_slots]]
            outgoing[window, slot] = jnp.where(low, first, second)
        return carry

    lax.fori_loop(0, WINDOWS, gather, 0)
    listed_ref[WINDOW] = outgoing[WINDOW]

    pl.semaphore_wait(barrier, total - 1)

    def halo(side):
        other = place(me - 1 if side == 0 else me + 1)
        start = 0 if side == 0 else columns - rim
        return [
            pltpu.make_async_remote_copy(
                src_ref=source.at[:, pl.ds(start, rim)],
                dst_ref=target.at[1 - side],
                send_sem=halo_send.at[side, kind],
                recv_sem=halo_recv.at[1 - side, kind],
                device_id=other,
                device_id_type=MESH,
            )
            for kind, (source, target) in enumerate([(dens_ref, halo_dens), (pack_ref, halo_pack)])
        ]

    @pl.when(me > 0)
    def _():
        for copy in halo(0):
            copy.start()

    @pl.when(me < total - 1)
    def _():
        for copy in halo(1):
            copy.start()

    def coarse_copy(other, slot):
        return pltpu.make_async_remote_copy(
            src_ref=coarse_ref.at[slot],
            dst_ref=coarse_ref.at[slot],
            send_sem=coarse_send.at[other],
            recv_sem=coarse_recv.at[slot],
            device_id=place(other),
            device_id_type=MESH,
        )

    def list_copy(window, landing):
        return pltpu.make_async_remote_copy(
            src_ref=outgoing.at[window],
            dst_ref=listed_ref.at[landing],
            send_sem=list_send.at[window],
            recv_sem=list_recv.at[landing],
            device_id=place(me + window - WINDOW),
            device_id_type=MESH,
        )

    def in_window(window):
        other = me + window - WINDOW
        return (window != WINDOW) & (other >= 0) & (other < total)

    def send_list(window, carry):
        @pl.when(in_window(window))
        def _():
            list_copy(window, 2 * WINDOW - window).start()

        return carry

    def send_coarse(step, carry):
        coarse_copy((me + step) % total, me).start()
        return carry

    lax.fori_loop(1, total, send_coarse, 0)
    lax.fori_loop(0, WINDOWS, send_list, 0)

    batch = 4

    def prepare(first_leaf, pack, dens, own):
        left, right = features(pack)
        right = right.astype(jnp.bfloat16)
        for k in range(batch):
            part = slice(k * leaf_size, (k + 1) * leaf_size)
            col_feat[first_leaf + k] = right[:, part]
            values[first_leaf + k] = dens[:, part]
            if own:
                row_feat[first_leaf - REACH + k] = left[:, part].T.astype(jnp.bfloat16)

    def prepare_own(step, carry):
        span = pl.ds(pl.multiple_of(step * batch * leaf_size, batch * leaf_size), batch * leaf_size)
        prepare(REACH + step * batch, pack_ref[:, span], dens_ref[:, span], True)
        return carry

    lax.fori_loop(0, leaf_count // batch, prepare_own, 0)

    def near_leaf(leaf, carry):
        mine = row_feat[leaf]
        field = jnp.zeros((dens_ref.shape[0], leaf_size), jnp.float32)
        partners = [leaf + REACH + offsets_ref[leaf, slot] for slot in range(slots)]
        for first in range(0, slots, 2):
            some = partners[first : first + 2]
            cols = jnp.concatenate([col_feat[p] for p in some], axis=1)
            vals = jnp.concatenate([values[p] for p in some], axis=1)
            kernel = lax.rsqrt(dot(mine, cols, PLAIN)).astype(jnp.bfloat16)
            field = field + dot(vals, kernel, ROWS_BY_ROWS)
        near_ref[:, pl.ds(pl.multiple_of(leaf * leaf_size, leaf_size), leaf_size)] = field
        return carry

    lax.fori_loop(REACH, leaf_count - REACH, near_leaf, 0)

    @pl.when(me == 0)
    def _():
        halo_dens[0] = jnp.zeros(halo_dens.shape[1:], halo_dens.dtype)
        halo_pack[0] = jnp.ones(halo_pack.shape[1:], halo_pack.dtype)

    @pl.when(me == total - 1)
    def _():
        halo_dens[1] = jnp.zeros(halo_dens.shape[1:], halo_dens.dtype)
        halo_pack[1] = jnp.ones(halo_pack.shape[1:], halo_pack.dtype)

    @pl.when(me > 0)
    def _():
        for copy in halo(1):
            copy.wait_recv()
        for copy in halo(0):
            copy.wait_send()

    @pl.when(me < total - 1)
    def _():
        for copy in halo(0):
            copy.wait_recv()
        for copy in halo(1):
            copy.wait_send()

    for side in range(2):
        base = 0 if side == 0 else REACH + leaf_count

        def prepare_rim(step, carry, side=side, base=base):
            width = batch * leaf_size
            span = pl.ds(pl.multiple_of(step * width, width), width)
            prepare(base + step * batch, halo_pack[side, :, span], halo_dens[side, :, span], False)
            return carry

        lax.fori_loop(0, REACH // batch, prepare_rim, 0)

    lax.fori_loop(0, REACH, near_leaf, 0)
    lax.fori_loop(leaf_count - REACH, leaf_count, near_leaf, 0)

    def end_coarse(step, carry):
        other = (me + step) % total
        coarse_copy(other, other).wait_recv()
        coarse_copy(other, me).wait_send()
        return carry

    lax.fori_loop(1, total, end_coarse, 0)

    def end_list(window, carry):
        @pl.when(in_window(window))
        def _():
            list_copy(window, window).wait_recv()
            list_copy(window, 2 * WINDOW - window).wait_send()

        return carry

    lax.fori_loop(0, WINDOWS, end_list, 0)


def exchange(sizes, offsets, lists, densities, pack, leaf_basis, transfer):
    rhs, columns = densities.shape
    leaf_count, rank, leaf_size = leaf_basis.shape
    total = sizes[0] * sizes[1]
    groups = leaf_count // CHILDREN
    half_slots = lists.shape[1] // 2
    vmem = pl.BlockSpec(memory_space=pltpu.VMEM)
    smem = pl.BlockSpec(memory_space=pltpu.SMEM)
    rim = REACH * leaf_size
    dma = pltpu.SemaphoreType.DMA
    return pl.pallas_call(
        functools.partial(exchange_kernel, sizes),
        out_shape=(
            jax.ShapeDtypeStruct((rhs, columns), jnp.float32),
            jax.ShapeDtypeStruct((WINDOWS, half_slots, rhs, 2 * rank), jnp.bfloat16),
            jax.ShapeDtypeStruct((total, groups // 2, rhs, 2 * rank), jnp.bfloat16),
        ),
        in_specs=[smem, smem, vmem, vmem, vmem, vmem],
        out_specs=(vmem, vmem, vmem),
        scratch_shapes=[
            pltpu.VMEM((leaf_count, leaf_size, 48), jnp.bfloat16),
            pltpu.VMEM((leaf_count + 2 * REACH, 48, leaf_size), jnp.bfloat16),
            pltpu.VMEM((leaf_count + 2 * REACH, rhs, leaf_size), jnp.bfloat16),
            pltpu.VMEM((leaf_count, rhs, 2 * rank), jnp.bfloat16),
            pltpu.VMEM((WINDOWS, half_slots, rhs, 2 * rank), jnp.bfloat16),
            pltpu.VMEM((2, rhs, rim), jnp.bfloat16),
            pltpu.VMEM((2, 8, rim), jnp.float32),
            dma((2, 2)),
            dma((2, 2)),
            dma((WINDOWS,)),
            dma((WINDOWS,)),
            dma((total,)),
            dma((total,)),
        ],
        compiler_params=pltpu.CompilerParams(
            collective_id=0, has_side_effects=True, vmem_limit_bytes=32 * 1024 * 1024
        ),
        name="exchange",
    )(offsets, lists, densities, pack, leaf_basis, transfer)


def far_kernel(
    relay_ref,
    refs_ref,
    listed_ref,
    coarse_ref,
    coupling_ref,
    coarse_coupling_ref,
    transfer_ref,
    basis_ref,
    near_ref,
    out_ref,
    listed,
    coarse,
):
    step = pl.program_id(0)
    rank, leaf_size = basis_ref.shape[1:]
    rhs = near_ref.shape[0]
    low = lax.broadcasted_iota(jnp.int32, (rhs, 2 * rank), 1) < rank

    @pl.when(step == 0)
    def _():
        half = listed_ref.shape[1]

        def open_list(window, carry):
            for slot in range(half):
                both = listed_ref[window, slot].astype(jnp.float32)
                turned = pltpu.roll(both, rank, 1)
                index = window * 2 * half + slot
                listed[index] = jnp.where(low, both, turned).astype(jnp.bfloat16)
                listed[index + half] = jnp.where(low, turned, both).astype(jnp.bfloat16)
            return carry

        lax.fori_loop(0, listed_ref.shape[0], open_list, 0)
        pairs = coarse_ref.shape[1]

        def open_coarse(owner, carry):
            for k in range(4 * pairs):
                both = coarse_ref[owner * 4 + k // pairs, k % pairs].astype(jnp.float32)
                turned = pltpu.roll(both, rank, 1)
                index = owner * 8 * pairs + 2 * k
                coarse[index] = jnp.where(low, both, turned).astype(jnp.bfloat16)
                coarse[index + 1] = jnp.where(low, turned, both).astype(jnp.bfloat16)
            return carry

        lax.fori_loop(0, coarse_ref.shape[0] // 4, open_coarse, 0)

    def couple(blocks, store, pick, count):
        total = jnp.zeros((rhs, rank), jnp.float32)
        for slot in range(0, count, 4):
            matrix = jnp.concatenate([blocks(slot + k) for k in range(4)], axis=1)
            taken = [store[pick(slot + k)] for k in range(4)]
            picked = jnp.concatenate(
                [jnp.where(low, taken[0], taken[1]), jnp.where(low, taken[2], taken[3])], axis=1
            )
            total = total + dot(picked, matrix, ROWS_BY_ROWS)
        return total

    local1 = couple(
        lambda s: coarse_coupling_ref[0, s], coarse, lambda s: refs_ref[step, s], refs_ref.shape[1]
    ).astype(jnp.bfloat16)

    def one_leaf(child, carry):
        leaf = step * CHILDREN + child
        local0 = couple(
            lambda s: coupling_ref[child, s], listed, lambda s: relay_ref[leaf, s], relay_ref.shape[1]
        )
        downward = dot(local1, transfer_ref[child], ROWS_BY_ROWS)
        field = (local0 + downward).astype(jnp.bfloat16)
        span = pl.ds(pl.multiple_of(child * leaf_size, leaf_size), leaf_size)
        out_ref[:, span] = near_ref[:, span] + dot(field, basis_ref[child], PLAIN)
        return carry

    lax.fori_loop(0, CHILDREN, one_leaf, 0, unroll=2)


def far(relay_refs, coarse_refs, listed, everyone, coupling, coarse_coupling, transfer, basis, near):
    leaf_count, rank, leaf_size = basis.shape
    rhs = near.shape[0]
    groups = leaf_count // CHILDREN
    width = CHILDREN * leaf_size
    vmem = pl.BlockSpec(memory_space=pltpu.VMEM)
    smem = pl.BlockSpec(memory_space=pltpu.SMEM)
    return pl.pallas_call(
        far_kernel,
        grid=(groups,),
        out_shape=jax.ShapeDtypeStruct(near.shape, jnp.float32),
        in_specs=[
            smem,
            smem,
            vmem,
            vmem,
            pl.BlockSpec((CHILDREN,) + coupling.shape[1:], lambda q: (q, 0, 0, 0)),
            pl.BlockSpec((1,) + coarse_coupling.shape[1:], lambda q: (q, 0, 0, 0)),
            pl.BlockSpec((CHILDREN, rank, rank), lambda q: (q, 0, 0)),
            pl.BlockSpec((CHILDREN, rank, leaf_size), lambda q: (q, 0, 0)),
            pl.BlockSpec((rhs, width), lambda q: (0, q)),
        ],
        out_specs=pl.BlockSpec((rhs, width), lambda q: (0, q)),
        scratch_shapes=[
            pltpu.VMEM((listed.shape[0] * listed.shape[1] * 2, rhs, 2 * rank), jnp.bfloat16),
            pltpu.VMEM((everyone.shape[0] * everyone.shape[1] * 2, rhs, 2 * rank), jnp.bfloat16),
        ],
        compiler_params=pltpu.CompilerParams(vmem_limit_bytes=40 * 1024 * 1024),
        name="far",
    )(relay_refs, coarse_refs, listed, everyone, coupling, coarse_coupling, transfer, basis, near)


def local(
    sizes,
    densities,
    points,
    weights,
    near_offsets,
    leaf_basis,
    transfer,
    send_lists,
    relay_refs,
    leaf_coupling,
    coarse_refs,
    coarse_coupling,
):
    pack = jnp.concatenate([points, jnp.broadcast_to(weights[None, :], (5, weights.shape[0]))], axis=0)
    near, listed, everyone = exchange(
        sizes, near_offsets, send_lists[0], densities, pack, leaf_basis, transfer
    )
    return far(
        relay_refs,
        coarse_refs,
        listed,
        everyone,
        leaf_coupling,
        coarse_coupling,
        transfer,
        leaf_basis,
        near,
    )


def solution(mesh):
    sizes = (mesh.shape["gx"], mesh.shape["gy"])
    in_specs = (
        P(None, ("gx", "gy")),
        P(None, ("gx", "gy")),
        P(("gx", "gy")),
        P(("gx", "gy"), None),
        P(("gx", "gy"), None, None),
        P(("gx", "gy"), None, None),
        P(("gx", "gy"), None, None),
        P(("gx", "gy"), None),
        P(("gx", "gy"), None, None, None),
        P(("gx", "gy"), None),
        P(("gx", "gy"), None, None, None),
    )
    out_specs = P(None, ("gx", "gy"))
    return jax.shard_map(
        functools.partial(local, sizes),
        mesh=mesh,
        in_specs=in_specs,
        out_specs=out_specs,
        check_vma=False,
    )
```

time: 201 us -> 66 us (0.33); the launches traced: 197 us -> 65.4 us
  Pallas kernels: 0 us -> 54.1 us
  starting transfers between devices: 43.9 us -> 0 us
  matrix products: 42.8 us -> 0 us
  blocking collectives: 38.6 us -> 0 us
  local copies, waits for them, and re-layouts: 42 us -> 10.3 us
  waiting for transfers between devices: 13.2 us -> 0 us
  other arithmetic: 13.5 us -> 0.88 us
  loops' own time: 2.91 us -> 0 us
    pallas_call x0 -> x2, Pallas kernels: none -> 54.2 us  [the longest x1 36.6 us: exchange(): pl.pallas_call(functools.partial(exchange_kernel, sizes), out_shape=(jax....]
    ppermute x18 -> x0, starting transfers between devices: 43.9 us -> none  [from_behind(): return lax.ppermute(shard, axis, pairs)]
    dot_general x8 -> x0, matrix products: 42.8 us -> none  [the longest x4 27.8 us: near_block(): jnp.einsum('lisj,rlsj->rli', kernel, partner_values, preferred_element_ty...]
    all_gather x1 -> x0, blocking collectives: 38.6 us -> none  [local(): everyone = lax.all_gather(coeff1, ('gx', 'gy'), axis=0, tiled=True)]
    gather x7 -> x0, local copies, waits for them, and re-layouts: 18.8 us -> none  [the longest x1 8.46 us: local(): picked = jnp.take(received, relay_refs, axis=0)]
    ppermute x18 -> x0, waiting for transfers between devices: 13.2 us -> none  [from_behind(): return lax.ppermute(shard, axis, pairs)]
    while x9 -> x0, local copies, waits for them, and re-layouts: 5.23 us -> none
    and x7 -> x0, other arithmetic: 4.64 us -> none  [the longest x4 2.75 us: near_block(): partner_data = jnp.take(extended, partner_rows, axis=1)]
  transfers between devices with their start and end apart: 18 -> 0, of which waited for: 5 -> 0; matrix products, arithmetic and copies ran while one was open for 19% -> 0% of each run, Pallas kernels for 0% -> 0%
where the time goes in v1:
time: 66 us; the launch traced here: 65.4 us
  Pallas kernels  54.1 us (82%)
  local copies, waits for them, and re-layouts  10.3 us (16%)
  other arithmetic  0.88 us (1%)
    pallas_call x1, Pallas kernels, exchange(): pl.pallas_call(functools.partial(exchange_kernel, sizes), out_shape=(jax....  36.6 us
    pallas_call x1, Pallas kernels, far(): pl.pallas_call(far_kernel, grid=(groups,), out_shape=jax.ShapeDtypeStruct...  17.5 us
    unnamed x18, local copies, waits for them, and re-layouts  9.6 us

profile of v1, /device:TPU:0, one launch (start us, length us, event | category | flops | bytes accessed | tf_op | source)
XLA Modules:
  0.0 65.4 jit_solution(725125376033393239)
XLA Ops:
  0.0 0.8 %copy.12 = s32[1,17,16]{2,1,0:T(8,128)S(1)} copy(s32[1,17,16]{1,2,0:T(8,128)} %param.17) | data formatting | bytes 2176 | tf_op args[6]
  0.8 0.8 %copy.13.offsets_ref = s32[32,13]{1,0:T(8,128)S(1)} copy(s32[32,13]{0,1:T(8,128)} %param.14) | data formatting | bytes 3328 | tf_op args[3]
  1.6 0.7 %broadcast_in_dim.2 = f32[5,4096]{1,0:T(8,128)S(1)} broadcast(f32[4096]{0:T(1024)} %param.13), dimensions={1} | broadcast | bytes 98304 | tf_op jit(solution)/shard_map/broadcast_in_dim | solution.py:453
  2.3 0.9 %pad_maximum_fusion.pack_ref = f32[8,4096]{1,0:T(8,128)S(1)} fusion(f32[5,4096]{1,0:T(8,128)S(1)} %broadcast_in_dim.2, f32[3,4096]{1,0:T(4,128)} %param.12), kind=kLoop, calls=%fused_computation | loop fusion | flops 32768 | bytes 262144 | tf_op jit(solution)/shard_map/concatenate | solution.py:453
  3.2 0.0 copy-start.1
  3.2 1.0 %copy-done.1 = bf16[32,64,128]{2,1,0:T(8,128)(2,1)S(1)} copy-done((bf16[32,64,128]{2,1,0:T(8,128)(2,1)S(1)}, bf16[32,64,128]{2,1,0:T(8,128)(2,1)}, u32[]{:S(2)}) %copy-start.1) | copy-done | bytes 524312
  4.2 0.0 copy-start.3
  4.2 1.0 %copy-done.3 = bf16[32,64,64]{2,1,0:T(8,128)(2,1)S(1)} copy-done((bf16[32,64,64]{2,1,0:T(8,128)(2,1)S(1)}, bf16[32,64,64]{2,1,0:T(8,128)(2,1)}, u32[]{:S(2)}) %copy-start.3) | copy-done | bytes 262168
  5.3 0.0 copy-start.5
  5.3 0.9 %copy-done.5 = bf16[16,4096]{1,0:T(8,128)(2,1)S(1)} copy-done((bf16[16,4096]{1,0:T(8,128)(2,1)S(1)}, bf16[16,4096]{1,0:T(8,128)(2,1)}, u32[]{:S(2)}) %copy-start.5) | copy-done | bytes 131096
  6.2 36.6 %exchange.1 = (f32[16,4096]{1,0:T(8,128)S(1)}, bf16[17,8,16,128]{3,2,1,0:T(8,128)(2,1)S(1)}, bf16[32,2,16,128]{3,2,1,0:T(8,128)(2,1)S(1)}) custom-call(s32[32,13]{1,0:T(8,128)S(1)} %copy.13.offsets_ref, s32[17,16]{1,0:T(8,128)S(1)} %bitcast.1, bf16[16,4096]{1,0:T(8,128)(2,1)S(1)} %copy-done.5, f32[8,4096]{1,0:T(8,128)S(1)} %pad_maximum_fusion.pack_ref, ...), custom_call_target="tpu_custom_call" | custom-call | tf_op jit(solution)/shard_map/exchange/pallas_call | solution.py:301
  42.8 0.0 copy-start
  42.8 1.6 %copy-done = bf16[4,32,64,64]{3,2,1,0:T(8,128)(2,1)S(1)} copy-done((bf16[4,32,64,64]{3,2,1,0:T(8,128)(2,1)S(1)}, bf16[4,32,64,64]{3,2,1,0:T(8,128)(2,1)}, u32[]{:S(2)}) %copy-start) | copy-done | bytes 1048600
  44.4 0.0 copy-start.2
  44.4 1.0 %copy-done.2 = bf16[32,64,128]{2,1,0:T(8,128)(2,1)S(1)} copy-done((bf16[32,64,128]{2,1,0:T(8,128)(2,1)S(1)}, bf16[32,64,128]{2,1,0:T(8,128)(2,1)}, u32[]{:S(2)}) %copy-start.2) | copy-done | bytes 524312
  45.4 0.0 copy-start.4
  45.4 1.0 %copy-done.4 = bf16[32,64,64]{2,1,0:T(8,128)(2,1)S(1)} copy-done((bf16[32,64,64]{2,1,0:T(8,128)(2,1)S(1)}, bf16[32,64,64]{2,1,0:T(8,128)(2,1)}, u32[]{:S(2)}) %copy-start.4) | copy-done | bytes 262168
  46.5 0.0 copy-start.6
  46.5 0.7 %copy-done.6 = s32[32,32]{1,0:T(8,128)S(1)} copy-done((s32[32,32]{1,0:T(8,128)S(1)}, s32[32,32]{1,0:T(8,128)}, u32[]{:S(2)}) %copy-start.6) | copy-done | bytes 4120
  47.2 0.0 copy-start.7
  47.2 0.7 %copy-done.7 = s32[4,32]{1,0:T(4,128)S(1)} copy-done((s32[4,32]{1,0:T(4,128)S(1)}, s32[4,32]{1,0:T(4,128)}, u32[]{:S(2)}) %copy-start.7) | copy-done | bytes 536
  47.9 17.5 %far.1 = f32[16,4096]{1,0:T(8,128)} custom-call(s32[32,32]{1,0:T(8,128)S(1)} %copy-done.6, s32[4,32]{1,0:T(4,128)S(1)} %copy-done.7, bf16[17,8,16,128]{3,2,1,0:T(8,128)(2,1)S(1)} %get-tuple-element.8.listed_ref, bf16[32,2,16,128]{3,2,1,0:T(8,128)(2,1)S(1)} %get-tuple-element.9.coarse_ref, bf16[32,32,64,64]{3,2,1,0:T(8,128)(2,1)} %coupling_ref.1, ...), custom_call_target="tpu_custom_call" | custom-call | tf_op jit(solution)/shard_map/far/pallas_call | solution.py:414
Async XLA Ops:
  3.2 1.0 %copy-start.1 = (bf16[32,64,128]{2,1,0:T(8,128)(2,1)S(1)}, bf16[32,64,128]{2,1,0:T(8,128)(2,1)}, u32[]{:S(2)}) copy-start(bf16[32,64,128]{2,1,0:T(8,128)(2,1)} %basis_ref.3) | copy-start | bytes 1572868
  4.2 1.0 %copy-start.3 = (bf16[32,64,64]{2,1,0:T(8,128)(2,1)S(1)}, bf16[32,64,64]{2,1,0:T(8,128)(2,1)}, u32[]{:S(2)}) copy-start(bf16[32,64,64]{2,1,0:T(8,128)(2,1)} %transfer_ref.3) | copy-start | bytes 786436
  5.3 0.9 %copy-start.5 = (bf16[16,4096]{1,0:T(8,128)(2,1)S(1)}, bf16[16,4096]{1,0:T(8,128)(2,1)}, u32[]{:S(2)}) copy-start(bf16[16,4096]{1,0:T(8,128)(2,1)} %dens_ref.1) | copy-start | bytes 393220
  42.8 1.6 %copy-start = (bf16[4,32,64,64]{3,2,1,0:T(8,128)(2,1)S(1)}, bf16[4,32,64,64]{3,2,1,0:T(8,128)(2,1)}, u32[]{:S(2)}) copy-start(bf16[4,32,64,64]{3,2,1,0:T(8,128)(2,1)} %coarse_coupling_ref.1) | copy-start | bytes 3145732
  44.4 1.0 %copy-start.2 = (bf16[32,64,128]{2,1,0:T(8,128)(2,1)S(1)}, bf16[32,64,128]{2,1,0:T(8,128)(2,1)}, u32[]{:S(2)}) copy-start(bf16[32,64,128]{2,1,0:T(8,128)(2,1)} %basis_ref.3) | copy-start | bytes 1572868
  45.4 1.0 %copy-start.4 = (bf16[32,64,64]{2,1,0:T(8,128)(2,1)S(1)}, bf16[32,64,64]{2,1,0:T(8,128)(2,1)}, u32[]{:S(2)}) copy-start(bf16[32,64,64]{2,1,0:T(8,128)(2,1)} %transfer_ref.3) | copy-start | bytes 786436
  46.5 0.7 %copy-start.6 = (s32[32,32]{1,0:T(8,128)S(1)}, s32[32,32]{1,0:T(8,128)}, u32[]{:S(2)}) copy-start(s32[32,32]{1,0:T(8,128)} %relay_ref.1) | copy-start | bytes 12292
  47.2 0.7 %copy-start.7 = (s32[4,32]{1,0:T(4,128)S(1)}, s32[4,32]{1,0:T(4,128)}, u32[]{:S(2)}) copy-start(s32[4,32]{1,0:T(4,128)} %refs_ref.1) | copy-start | bytes 1540

commit v2 on v1

v2 whole, which is shorter than its diff:
```python
import functools
import math

import jax
import jax.numpy as jnp
from jax import lax
from jax.experimental import pallas as pl
from jax.experimental.pallas import tpu as pltpu
from jax.sharding import PartitionSpec as P

REACH = 8
WINDOW = 8
CHILDREN = 8
WINDOWS = 2 * WINDOW + 1

core_square = 0.0004
four_pi = 4.0 * math.pi

MESH = pl.DeviceIdType.MESH
ROWS_BY_ROWS = (((1,), (1,)), ((), ()))
PLAIN = (((1,), (0,)), ((), ()))


def dot(left, right, dims):
    return lax.dot_general(left, right, dims, preferred_element_type=jnp.float32)


def split(values):
    first = values.astype(jnp.bfloat16).astype(jnp.float32)
    rest = values - first
    second = rest.astype(jnp.bfloat16).astype(jnp.float32)
    return first, second, rest - second


def features(points, weights):
    row = lax.broadcasted_iota(jnp.int32, (8, points.shape[1]), 0)
    x, y, z = (points[k : k + 1] - 0.5 for k in range(3))
    norm = x * x + y * y + z * z
    root = four_pi / weights
    scale = root * root
    shifted = jnp.where(row == 0, x, jnp.where(row == 1, y, z))
    left = jnp.where(row < 3, shifted, jnp.where(row == 3, norm, jnp.where(row == 4, 1.0, 0.0)))
    right = scale * jnp.where(
        row < 3,
        -2.0 * shifted,
        jnp.where(row == 3, 1.0, jnp.where(row == 4, norm + core_square, 0.0)),
    )
    a1, a2, a3 = split(left)
    b1, b2, b3 = split(right)
    return (
        jnp.concatenate([a1, a1, a2, a1, a3, a2], axis=0),
        jnp.concatenate([b1, b2, b1, b3, b1, b2], axis=0),
    )


def whole_kernel(
    sizes,
    spans,
    table_ref,
    dens_any,
    points_any,
    weights_any,
    basis_any,
    transfer_any,
    coarse_coupling_any,
    coupling_any,
    out_ref,
    dens_ref,
    points_ref,
    weights_ref,
    basis_ref,
    transfer_ref,
    coarse_coupling_ref,
    coupling_ref,
    row_feat,
    col_feat,
    values,
    coeff,
    outgoing,
    listed_packed,
    coarse_packed,
    listed,
    coarse,
    local1,
    halo_dens,
    halo_points,
    halo_weights,
    load_sems,
    coupling_sems,
    halo_send,
    halo_recv,
    list_send,
    list_recv,
    coarse_send,
    coarse_recv,
):
    n_gx, n_gy = sizes
    total = n_gx * n_gy
    me = lax.axis_index("gx") * n_gy + lax.axis_index("gy")
    leaf_count, rank, leaf_size = basis_ref.shape
    rhs = dens_ref.shape[0]
    slots, far0, capacity, far1 = spans
    at_lists = slots
    at_relay = at_lists + capacity
    at_coarse = at_relay + leaf_count
    groups = leaf_count // CHILDREN
    half_slots = capacity // 2
    rim = REACH * leaf_size
    columns = leaf_count * leaf_size

    loads = [
        pltpu.make_async_copy(source, target, load_sems.at[k])
        for k, (source, target) in enumerate(
            [
                (dens_any, dens_ref),
                (basis_any, basis_ref),
                (transfer_any, transfer_ref),
                (points_any, points_ref),
                (weights_any, weights_ref),
                (coarse_coupling_any, coarse_coupling_ref),
            ]
        )
    ]
    for load in loads:
        load.start()

    def coupling_load(group):
        span = pl.ds(group * CHILDREN, CHILDREN)
        return pltpu.make_async_copy(
            coupling_any.at[span], coupling_ref.at[span], coupling_sems.at[group]
        )

    for group in range(groups):
        coupling_load(group).start()

    def place(index):
        return (index // n_gy, index % n_gy)

    barrier = pltpu.get_barrier_semaphore()

    def greet(step, carry):
        other = (me + step) % total
        pl.semaphore_signal(barrier, inc=1, device_id=place(other), device_id_type=MESH)
        return carry

    lax.fori_loop(1, total, greet, 0)
    for load in loads[:3]:
        load.wait()

    low = lax.broadcasted_iota(jnp.int32, (rhs, 2 * rank), 1) < rank

    def upward(pair, carry):
        parents = []
        for g in range(2):
            parent = None
            for child in range(CHILDREN):
                leaf = (pair * 2 + g) * CHILDREN + child
                start = pl.multiple_of(leaf * leaf_size, leaf_size)
                basis = basis_ref[leaf]
                doubled = jnp.concatenate([basis, basis], axis=0)
                both = dot(dens_ref[:, pl.ds(start, leaf_size)], doubled, ROWS_BY_ROWS)
                both = both.astype(jnp.bfloat16)
                coeff[leaf] = both
                term = dot(both[:, :rank], transfer_ref[leaf], PLAIN)
                parent = term if parent is None else parent + term
            parents.append(parent)
        coarse_packed[me, pair] = jnp.concatenate(parents, axis=1).astype(jnp.bfloat16)
        return carry

    lax.fori_loop(0, groups // 2, upward, 0)

    def gather(window, carry):
        for slot in range(half_slots):
            first = coeff[table_ref[at_lists + slot, window]]
            second = coeff[table_ref[at_lists + slot + half_slots, window]]
            outgoing[window, slot] = jnp.where(low, first, second)
        return carry

    lax.fori_loop(0, WINDOWS, gather, 0)
    listed_packed[WINDOW] = outgoing[WINDOW]
    loads[3].wait()
    loads[4].wait()

    pl.semaphore_wait(barrier, total - 1)

    def halo(side):
        other = place(me - 1 if side == 0 else me + 1)
        start = 0 if side == 0 else columns - rim
        leaf = 0 if side == 0 else leaf_count - REACH
        parts = [
            (dens_ref.at[:, pl.ds(start, rim)], halo_dens),
            (points_ref.at[:, pl.ds(start, rim)], halo_points),
            (weights_ref.at[pl.ds(leaf, REACH)], halo_weights),
        ]
        return [
            pltpu.make_async_remote_copy(
                src_ref=source,
                dst_ref=target.at[1 - side],
                send_sem=halo_send.at[side, kind],
                recv_sem=halo_recv.at[1 - side, kind],
                device_id=other,
                device_id_type=MESH,
            )
            for kind, (source, target) in enumerate(parts)
        ]

    @pl.when(me > 0)
    def _():
        for copy in halo(0):
            copy.start()

    @pl.when(me < total - 1)
    def _():
        for copy in halo(1):
            copy.start()

    def coarse_copy(other, slot):
        return pltpu.make_async_remote_copy(
            src_ref=coarse_packed.at[slot],
            dst_ref=coarse_packed.at[slot],
            send_sem=coarse_send.at[other],
            recv_sem=coarse_recv.at[slot],
            device_id=place(other),
            device_id_type=MESH,
        )

    def list_copy(window, landing):
        return pltpu.make_async_remote_copy(
            src_ref=outgoing.at[window],
            dst_ref=listed_packed.at[landing],
            send_sem=list_send.at[window],
            recv_sem=list_recv.at[landing],
            device_id=place(me + window - WINDOW),
            device_id_type=MESH,
        )

    def in_window(window):
        other = me + window - WINDOW
        return (window != WINDOW) & (other >= 0) & (other < total)

    def send_list(window, carry):
        @pl.when(in_window(window))
        def _():
            list_copy(window, 2 * WINDOW - window).start()

        return carry

    def send_coarse(step, carry):
        coarse_copy((me + step) % total, me).start()
        return carry

    lax.fori_loop(1, total, send_coarse, 0)
    lax.fori_loop(0, WINDOWS, send_list, 0)

    batch = 4

    def prepare(first_leaf, points, weights, dens, own):
        line = jnp.concatenate([weights[k : k + 1] for k in range(batch)], axis=1)
        left, right = features(points, line)
        right = right.astype(jnp.bfloat16)
        for k in range(batch):
            part = slice(k * leaf_size, (k + 1) * leaf_size)
            col_feat[first_leaf + k] = right[:, part]
            values[first_leaf + k] = dens[:, part]
            if own:
                row_feat[first_leaf - REACH + k] = left[:, part].T.astype(jnp.bfloat16)

    def prepare_own(step, carry):
        span = pl.ds(pl.multiple_of(step * batch * leaf_size, batch * leaf_size), batch * leaf_size)
        lines = weights_ref[pl.ds(step * batch, batch)]
        prepare(REACH + step * batch, points_ref[:, span], lines, dens_ref[:, span], True)
        return carry

    lax.fori_loop(0, leaf_count // batch, prepare_own, 0)

    def near_leaf(leaf, carry):
        mine = row_feat[leaf]
        field = jnp.zeros((leaf_size, rhs), jnp.float32)
        partners = [leaf + REACH + table_ref[slot, leaf] for slot in range(slots)]
        for first in range(0, slots, 2):
            some = partners[first : first + 2]
            cols = jnp.concatenate([col_feat[p] for p in some], axis=1)
            vals = jnp.concatenate([values[p] for p in some], axis=1)
            kernel = lax.rsqrt(dot(mine, cols, PLAIN)).astype(jnp.bfloat16)
            field = field + dot(kernel, vals, ROWS_BY_ROWS)
        out_ref[:, pl.ds(pl.multiple_of(leaf * leaf_size, leaf_size), leaf_size)] = field.T
        return carry

    lax.fori_loop(REACH, leaf_count - REACH, near_leaf, 0)

    @pl.when(me == 0)
    def _():
        halo_dens[0] = jnp.zeros(halo_dens.shape[1:], halo_dens.dtype)
        halo_points[0] = jnp.zeros(halo_points.shape[1:], halo_points.dtype)
        halo_weights[0] = jnp.ones(halo_weights.shape[1:], halo_weights.dtype)

    @pl.when(me == total - 1)
    def _():
        halo_dens[1] = jnp.zeros(halo_dens.shape[1:], halo_dens.dtype)
        halo_points[1] = jnp.zeros(halo_points.shape[1:], halo_points.dtype)
        halo_weights[1] = jnp.ones(halo_weights.shape[1:], halo_weights.dtype)

    @pl.when(me > 0)
    def _():
        for copy in halo(1):
            copy.wait_recv()
        for copy in halo(0):
            copy.wait_send()

    @pl.when(me < total - 1)
    def _():
        for copy in halo(0):
            copy.wait_recv()
        for copy in halo(1):
            copy.wait_send()

    for side in range(2):
        base = 0 if side == 0 else REACH + leaf_count

        def prepare_rim(step, carry, side=side, base=base):
            width = batch * leaf_size
            span = pl.ds(pl.multiple_of(step * width, width), width)
            lines = halo_weights[side, pl.ds(step * batch, batch)]
            dens = halo_dens[side, :, span]
            prepare(base + step * batch, halo_points[side, :, span], lines, dens, False)
            return carry

        lax.fori_loop(0, REACH // batch, prepare_rim, 0)

    lax.fori_loop(0, REACH, near_leaf, 0)
    lax.fori_loop(leaf_count - REACH, leaf_count, near_leaf, 0)

    def end_coarse(step, carry):
        other = (me + step) % total
        coarse_copy(other, other).wait_recv()
        coarse_copy(other, me).wait_send()
        return carry

    lax.fori_loop(1, total, end_coarse, 0)

    def opened(packed):
        both = packed.astype(jnp.float32)
        turned = pltpu.roll(both, rank, 1)
        return (
            jnp.where(low, both, turned).astype(jnp.bfloat16),
            jnp.where(low, turned, both).astype(jnp.bfloat16),
        )

    pairs = groups // 2

    def open_coarse(step, carry):
        for k in range(4 * pairs):
            first, second = opened(coarse_packed[step * 4 + k // pairs, k % pairs])
            index = step * 8 * pairs + 2 * k
            coarse[index] = first
            coarse[index + 1] = second
        return carry

    lax.fori_loop(0, total // 4, open_coarse, 0)
    loads[5].wait()

    def couple(blocks, store, pick, count):
        field = jnp.zeros((rank, rhs), jnp.float32)
        for slot in range(0, count, 4):
            matrix = jnp.concatenate([blocks(slot + k) for k in range(4)], axis=1)
            taken = [store[pick(slot + k)] for k in range(4)]
            picked = jnp.concatenate(
                [jnp.where(low, taken[0], taken[1]), jnp.where(low, taken[2], taken[3])], axis=1
            )
            field = field + dot(matrix, picked, ROWS_BY_ROWS)
        return field

    def one_group(group, carry):
        local1[group] = couple(
            lambda s: coarse_coupling_ref[group, s],
            coarse,
            lambda s: table_ref[at_coarse + group, s],
            far1,
        ).astype(jnp.bfloat16)
        return carry

    lax.fori_loop(0, groups, one_group, 0, unroll=2)

    def end_list(window, carry):
        @pl.when(in_window(window))
        def _():
            list_copy(window, window).wait_recv()
            list_copy(window, 2 * WINDOW - window).wait_send()

        return carry

    lax.fori_loop(0, WINDOWS, end_list, 0)

    def open_list(window, carry):
        for slot in range(half_slots):
            first, second = opened(listed_packed[window, slot])
            index = window * capacity + slot
            listed[index] = first
            listed[index + half_slots] = second
        return carry

    lax.fori_loop(0, WINDOWS, open_list, 0)

    for group in range(groups):
        coupling_load(group).wait()

    def one_leaf(leaf, carry):
        local0 = couple(
            lambda s: coupling_ref[leaf, s],
            listed,
            lambda s: table_ref[at_relay + leaf, s],
            far0,
        )
        downward = dot(transfer_ref[leaf], local1[leaf // CHILDREN], PLAIN)
        field = (local0 + downward).T.astype(jnp.bfloat16)
        span = pl.ds(pl.multiple_of(leaf * leaf_size, leaf_size), leaf_size)
        out_ref[:, span] = out_ref[:, span] + dot(field, basis_ref[leaf], PLAIN)
        return carry

    lax.fori_loop(0, leaf_count, one_leaf, 0, unroll=2)


def whole(sizes, spans, table, densities, points, weights, leaf_basis, transfer, coarse_coupling, coupling):
    rhs, columns = densities.shape
    leaf_count, rank, leaf_size = leaf_basis.shape
    total = sizes[0] * sizes[1]
    groups = leaf_count // CHILDREN
    capacity = spans[2]
    anywhere = pl.BlockSpec(memory_space=pl.ANY)
    rim = REACH * leaf_size
    dma = pltpu.SemaphoreType.DMA
    operands = (densities, points, weights, leaf_basis, transfer, coarse_coupling, coupling)
    held = [pltpu.VMEM(x.shape, x.dtype) for x in operands]
    half = jnp.bfloat16
    return pl.pallas_call(
        functools.partial(whole_kernel, sizes, spans),
        out_shape=jax.ShapeDtypeStruct((rhs, columns), jnp.float32),
        in_specs=[pl.BlockSpec(memory_space=pltpu.SMEM)] + [anywhere] * len(operands),
        out_specs=pl.BlockSpec(memory_space=pltpu.VMEM),
        scratch_shapes=held
        + [
            pltpu.VMEM((leaf_count, leaf_size, 48), half),
            pltpu.VMEM((leaf_count + 2 * REACH, 48, leaf_size), half),
            pltpu.VMEM((leaf_count + 2 * REACH, rhs, leaf_size), half),
            pltpu.VMEM((leaf_count, rhs, 2 * rank), half),
            pltpu.VMEM((WINDOWS, capacity // 2, rhs, 2 * rank), half),
            pltpu.VMEM((WINDOWS, capacity // 2, rhs, 2 * rank), half),
            pltpu.VMEM((total, groups // 2, rhs, 2 * rank), half),
            pltpu.VMEM((WINDOWS * capacity, rhs, 2 * rank), half),
            pltpu.VMEM((total * groups, rhs, 2 * rank), half),
            pltpu.VMEM((groups, rank, rhs), half),
            pltpu.VMEM((2, rhs, rim), half),
            pltpu.VMEM((2, 3, rim), jnp.float32),
            pltpu.VMEM((2, REACH, leaf_size), jnp.float32),
            dma((6,)),
            dma((groups,)),
            dma((2, 3)),
            dma((2, 3)),
            dma((WINDOWS,)),
            dma((WINDOWS,)),
            dma((total,)),
            dma((total,)),
        ],
        compiler_params=pltpu.CompilerParams(
            collective_id=0, has_side_effects=True, vmem_limit_bytes=63 * 1024 * 1024
        ),
        name="whole",
    )(table, *operands)


def local(
    sizes,
    densities,
    points,
    weights,
    near_offsets,
    leaf_basis,
    transfer,
    send_lists,
    relay_refs,
    leaf_coupling,
    coarse_refs,
    coarse_coupling,
):
    leaf_count, _, leaf_size = leaf_basis.shape
    lines = weights.reshape(leaf_count, leaf_size)
    tables = [near_offsets.T, send_lists[0].T, relay_refs, coarse_refs]
    width = max(array.shape[1] for array in tables)
    table = jnp.concatenate(
        [jnp.pad(array, ((0, 0), (0, width - array.shape[1]))) for array in tables], axis=0
    )
    spans = (
        near_offsets.shape[1],
        relay_refs.shape[1],
        send_lists.shape[2],
        coarse_refs.shape[1],
    )
    return whole(
        sizes,
        spans,
        table,
        densities,
        points,
        lines,
        leaf_basis,
        transfer,
        coarse_coupling,
        leaf_coupling,
    )


def solution(mesh):
    sizes = (mesh.shape["gx"], mesh.shape["gy"])
    in_specs = (
        P(None, ("gx", "gy")),
        P(None, ("gx", "gy")),
        P(("gx", "gy")),
        P(("gx", "gy"), None),
        P(("gx", "gy"), None, None),
        P(("gx", "gy"), None, None),
        P(("gx", "gy"), None, None),
        P(("gx", "gy"), None),
        P(("gx", "gy"), None, None, None),
        P(("gx", "gy"), None),
        P(("gx", "gy"), None, None, None),
    )
    out_specs = P(None, ("gx", "gy"))
    return jax.shard_map(
        functools.partial(local, sizes),
        mesh=mesh,
        in_specs=in_specs,
        out_specs=out_specs,
        check_vma=False,
    )
```

time: 66 us -> 48.3 us (0.73)
  Pallas kernels: 54.1 us -> 44.9 us
  local copies, waits for them, and re-layouts: 10.3 us -> 1.67 us
    pallas_call x2 -> x1, Pallas kernels: 54.2 us -> 44.9 us  [whole(): pl.pallas_call(functools.partial(whole_kernel, sizes, spans), out_shape=j...]
    unnamed x18 -> x1, local copies, waits for them, and re-layouts: 9.6 us -> 1.67 us
    broadcast_in_dim x1 -> x0, local copies, waits for them, and re-layouts: 0.73 us -> none  [local(): jnp.broadcast_to(weights[None, :], (5, weights.shape[0]))]
where the time goes in v2:
time: 48.3 us; the launch traced here: 48 us
  Pallas kernels  44.9 us (93%)
  local copies, waits for them, and re-layouts  1.67 us (3%)
  other arithmetic  1.38 us (3%)
    pallas_call x1, Pallas kernels, whole(): pl.pallas_call(functools.partial(whole_kernel, sizes, spans), out_shape=j...  44.9 us
    unnamed x1, local copies, waits for them, and re-layouts  1.67 us
    concatenate x1, other arithmetic, local(): jnp.concatenate([jnp.pad(array, ((0, 0), (0, width - array.shape[1]))) fo...  1.38 us

profile of v2, /device:TPU:0, one launch (start us, length us, event | category | flops | bytes accessed | tf_op | source)
XLA Modules:
  0.0 48.0 jit_solution(6974669047562339518)
XLA Ops:
  0.0 1.4 %fusion.1.table_ref = s32[65,32]{1,0:T(8,128)} fusion(s32[16,17]{1,0:T(8,128)} %bitcast.6, s32[4,32]{1,0:T(4,128)} %param.20, s32[32,32]{1,0:T(8,128)} %param.18, s32[13,32]{1,0:T(8,128)} %bitcast.7), kind=kLoop, calls=%fused_computation.2 | loop fusion | flops 6240 | bytes 15680 | tf_op jit(solution)/shard_map/concatenate | solution.py:489
  1.4 44.9 %whole.1 = f32[16,4096]{1,0:T(8,128)} custom-call(s32[65,32]{1,0:T(8,128)} %fusion.1.table_ref, bf16[16,4096]{1,0:T(8,128)(2,1)} %dens_any.1, f32[3,4096]{1,0:T(4,128)} %points_any.1, f32[32,128]{1,0:T(8,128)} %bitcast.5, bf16[32,64,128]{2,1,0:T(8,128)(2,1)} %basis_any.1, bf16[32,64,64]{2,1,0:T(8,128)(2,1)} %transfer_any.1, ...), custom_call_target="tpu_custom_call" | custom-call | tf_op jit(solution)/shard_map/whole/pallas_call | solution.py:435
  46.3 1.7 %copy.18 = f32[16,4096]{1,0:T(8,128)} copy(f32[16,4096]{1,0:T(8,128)} %whole.1) | data formatting | bytes 524288

commit v3 on v2

--- a/solution.py
+++ b/solution.py
@@ -55,8 +55,10 @@
 
 def whole_kernel(
     sizes,
-    spans,
-    table_ref,
+    offsets_any,
+    lists_any,
+    relay_any,
+    refs_any,
     dens_any,
     points_any,
     weights_any,
@@ -65,6 +67,10 @@
     coarse_coupling_any,
     coupling_any,
     out_ref,
+    offsets_ref,
+    lists_ref,
+    relay_ref,
+    refs_ref,
     dens_ref,
     points_ref,
     weights_ref,
@@ -91,18 +97,18 @@
     halo_recv,
     list_send,
     list_recv,
-    coarse_send,
-    coarse_recv,
+    inner_send,
+    inner_recv,
+    outer_send,
+    outer_recv,
 ):
     n_gx, n_gy = sizes
     total = n_gx * n_gy
     me = lax.axis_index("gx") * n_gy + lax.axis_index("gy")
     leaf_count, rank, leaf_size = basis_ref.shape
     rhs = dens_ref.shape[0]
-    slots, far0, capacity, far1 = spans
-    at_lists = slots
-    at_relay = at_lists + capacity
-    at_coarse = at_relay + leaf_count
+    slots, capacity = offsets_ref.shape[0], lists_ref.shape[0]
+    far0, far1 = relay_ref.shape[1], refs_ref.shape[1]
     groups = leaf_count // CHILDREN
     half_slots = capacity // 2
     rim = REACH * leaf_size
@@ -112,11 +118,15 @@
         pltpu.make_async_copy(source, target, load_sems.at[k])
         for k, (source, target) in enumerate(
             [
+                (lists_any, lists_ref),
                 (dens_any, dens_ref),
                 (basis_any, basis_ref),
                 (transfer_any, transfer_ref),
                 (points_any, points_ref),
                 (weights_any, weights_ref),
+                (offsets_any, offsets_ref),
+                (refs_any, refs_ref),
+                (relay_any, relay_ref),
                 (coarse_coupling_any, coarse_coupling_ref),
             ]
         )
@@ -144,7 +154,7 @@
         return carry
 
     lax.fori_loop(1, total, greet, 0)
-    for load in loads[:3]:
+    for load in loads[:4]:
         load.wait()
 
     low = lax.broadcasted_iota(jnp.int32, (rhs, 2 * rank), 1) < rank
@@ -171,15 +181,15 @@
 
     def gather(window, carry):
         for slot in range(half_slots):
-            first = coeff[table_ref[at_lists + slot, window]]
-            second = coeff[table_ref[at_lists + slot + half_slots, window]]
+            first = coeff[lists_ref[slot, window]]
+            second = coeff[lists_ref[slot + half_slots, window]]
             outgoing[window, slot] = jnp.where(low, first, second)
         return carry
 
     lax.fori_loop(0, WINDOWS, gather, 0)
     listed_packed[WINDOW] = outgoing[WINDOW]
-    loads[3].wait()
-    loads[4].wait()
+    for load in loads[4:9]:
+        load.wait()
 
     pl.semaphore_wait(barrier, total - 1)
 
@@ -214,13 +224,27 @@
         for copy in halo(1):
             copy.start()
 
-    def coarse_copy(other, slot):
+    my_gx, my_gy = lax.axis_index("gx"), lax.axis_index("gy")
+
+    def inner_copy(other, slot):
+        block = coarse_packed.at[my_gx * n_gy + slot]
         return pltpu.make_async_remote_copy(
-            src_ref=coarse_packed.at[slot],
-            dst_ref=coarse_packed.at[slot],
-            send_sem=coarse_send.at[other],
-            recv_sem=coarse_recv.at[slot],
-            device_id=place(other),
+            src_ref=block,
+            dst_ref=block,
+            send_sem=inner_send.at[other],
+            recv_sem=inner_recv.at[slot],
+            device_id=(my_gx, other),
+            device_id_type=MESH,
+        )
+
+    def outer_copy(other, slot):
+        block = coarse_packed.at[pl.ds(slot * n_gy, n_gy)]
+        return pltpu.make_async_remote_copy(
+            src_ref=block,
+            dst_ref=block,
+            send_sem=outer_send.at[other],
+            recv_sem=outer_recv.at[slot],
+            device_id=(other, my_gy),
             device_id_type=MESH,
         )
 
@@ -245,11 +269,11 @@
 
         return carry
 
-    def send_coarse(step, carry):
-        coarse_copy((me + step) % total, me).start()
-        return carry
-
-    lax.fori_loop(1, total, send_coarse, 0)
+    def send_inner(step, carry):
+        inner_copy((my_gy + step) % n_gy, my_gy).start()
+        return carry
+
+    lax.fori_loop(1, n_gy, send_inner, 0)
     lax.fori_loop(0, WINDOWS, send_list, 0)
 
     batch = 4
@@ -276,7 +300,7 @@
     def near_leaf(leaf, carry):
         mine = row_feat[leaf]
         field = jnp.zeros((leaf_size, rhs), jnp.float32)
-        partners = [leaf + REACH + table_ref[slot, leaf] for slot in range(slots)]
+        partners = [leaf + REACH + offsets_ref[slot, leaf] for slot in range(slots)]
         for first in range(0, slots, 2):
             some = partners[first : first + 2]
             cols = jnp.concatenate([col_feat[p] for p in some], axis=1)
@@ -286,7 +310,23 @@
         out_ref[:, pl.ds(pl.multiple_of(leaf * leaf_size, leaf_size), leaf_size)] = field.T
         return carry
 
-    lax.fori_loop(REACH, leaf_count - REACH, near_leaf, 0)
+    middle = leaf_count // 2
+    lax.fori_loop(REACH, middle, near_leaf, 0, unroll=2)
+
+    def end_inner(step, carry):
+        other = (my_gy + step) % n_gy
+        inner_copy(other, other).wait_recv()
+        inner_copy(other, my_gy).wait_send()
+        return carry
+
+    lax.fori_loop(1, n_gy, end_inner, 0)
+
+    def send_outer(step, carry):
+        outer_copy((my_gx + step) % n_gx, my_gx).start()
+        return carry
+
+    lax.fori_loop(1, n_gx, send_outer, 0)
+    lax.fori_loop(middle, leaf_count - REACH, near_leaf, 0, unroll=2)
 
     @pl.when(me == 0)
     def _():
@@ -327,16 +367,16 @@
 
         lax.fori_loop(0, REACH // batch, prepare_rim, 0)
 
-    lax.fori_loop(0, REACH, near_leaf, 0)
-    lax.fori_loop(leaf_count - REACH, leaf_count, near_leaf, 0)
-
-    def end_coarse(step, carry):
-        other = (me + step) % total
-        coarse_copy(other, other).wait_recv()
-        coarse_copy(other, me).wait_send()
-        return carry
-
-    lax.fori_loop(1, total, end_coarse, 0)
+    lax.fori_loop(0, REACH, near_leaf, 0, unroll=2)
+    lax.fori_loop(leaf_count - REACH, leaf_count, near_leaf, 0, unroll=2)
+
+    def end_outer(step, carry):
+        other = (my_gx + step) % n_gx
+        outer_copy(other, other).wait_recv()
+        outer_copy(other, my_gx).wait_send()
+        return carry
+
+    lax.fori_loop(1, n_gx, end_outer, 0)
 
     def opened(packed):
         both = packed.astype(jnp.float32)
@@ -357,7 +397,7 @@
         return carry
 
     lax.fori_loop(0, total // 4, open_coarse, 0)
-    loads[5].wait()
+    loads[9].wait()
 
     def couple(blocks, store, pick, count):
         field = jnp.zeros((rank, rhs), jnp.float32)
@@ -374,7 +414,7 @@
         local1[group] = couple(
             lambda s: coarse_coupling_ref[group, s],
             coarse,
-            lambda s: table_ref[at_coarse + group, s],
+            lambda s: refs_ref[group, s],
             far1,
         ).astype(jnp.bfloat16)
         return carry
@@ -408,7 +448,7 @@
         local0 = couple(
             lambda s: coupling_ref[leaf, s],
             listed,
-            lambda s: table_ref[at_relay + leaf, s],
+            lambda s: relay_ref[leaf, s],
             far0,
         )
         downward = dot(transfer_ref[leaf], local1[leaf // CHILDREN], PLAIN)
@@ -420,22 +460,23 @@
     lax.fori_loop(0, leaf_count, one_leaf, 0, unroll=2)
 
 
-def whole(sizes, spans, table, densities, points, weights, leaf_basis, transfer, coarse_coupling, coupling):
+def whole(sizes, tables, densities, points, weights, leaf_basis, transfer, coarse_coupling, coupling):
     rhs, columns = densities.shape
     leaf_count, rank, leaf_size = leaf_basis.shape
     total = sizes[0] * sizes[1]
     groups = leaf_count // CHILDREN
-    capacity = spans[2]
+    capacity = tables[1].shape[0]
     anywhere = pl.BlockSpec(memory_space=pl.ANY)
     rim = REACH * leaf_size
     dma = pltpu.SemaphoreType.DMA
     operands = (densities, points, weights, leaf_basis, transfer, coarse_coupling, coupling)
-    held = [pltpu.VMEM(x.shape, x.dtype) for x in operands]
+    held = [pltpu.SMEM(x.shape, x.dtype) for x in tables]
+    held += [pltpu.VMEM(x.shape, x.dtype) for x in operands]
     half = jnp.bfloat16
     return pl.pallas_call(
-        functools.partial(whole_kernel, sizes, spans),
+        functools.partial(whole_kernel, sizes),
         out_shape=jax.ShapeDtypeStruct((rhs, columns), jnp.float32),
-        in_specs=[pl.BlockSpec(memory_space=pltpu.SMEM)] + [anywhere] * len(operands),
+        in_specs=[anywhere] * (len(tables) + len(operands)),
         out_specs=pl.BlockSpec(memory_space=pltpu.VMEM),
         scratch_shapes=held
         + [
@@ -452,20 +493,22 @@
             pltpu.VMEM((2, rhs, rim), half),
             pltpu.VMEM((2, 3, rim), jnp.float32),
             pltpu.VMEM((2, REACH, leaf_size), jnp.float32),
-            dma((6,)),
+            dma((10,)),
             dma((groups,)),
             dma((2, 3)),
             dma((2, 3)),
             dma((WINDOWS,)),
             dma((WINDOWS,)),
-            dma((total,)),
-            dma((total,)),
+            dma((sizes[1],)),
+            dma((sizes[1],)),
+            dma((sizes[0],)),
+            dma((sizes[0],)),
         ],
         compiler_params=pltpu.CompilerParams(
             collective_id=0, has_side_effects=True, vmem_limit_bytes=63 * 1024 * 1024
         ),
         name="whole",
-    )(table, *operands)
+    )(*tables, *operands)
 
 
 def local(
@@ -484,21 +527,10 @@
 ):
     leaf_count, _, leaf_size = leaf_basis.shape
     lines = weights.reshape(leaf_count, leaf_size)
-    tables = [near_offsets.T, send_lists[0].T, relay_refs, coarse_refs]
-    width = max(array.shape[1] for array in tables)
-    table = jnp.concatenate(
-        [jnp.pad(array, ((0, 0), (0, width - array.shape[1]))) for array in tables], axis=0
-    )
-    spans = (
-        near_offsets.shape[1],
-        relay_refs.shape[1],
-        send_lists.shape[2],
-        coarse_refs.shape[1],
-    )
+    tables = (near_offsets.T, send_lists[0].T, relay_refs, coarse_refs)
     return whole(
         sizes,
-        spans,
-        table,
+        tables,
         densities,
         points,
         lines,

time: 48.3 us -> 43.8 us (0.907)
  Pallas kernels: 44.9 us -> 41.9 us
  other arithmetic: 1.38 us -> 0 us
    pallas_call x1, Pallas kernels: 44.9 us -> 41.9 us  [whole(): pl.pallas_call(functools.partial(whole_kernel, sizes), out_shape=jax.Shap...]
    concatenate x1 -> x0, other arithmetic: 1.38 us -> none  [local(): jnp.concatenate([jnp.pad(array, ((0, 0), (0, width - array.shape[1]))) fo...]
where the time goes in v3:
time: 43.8 us; the launch traced here: 43.6 us
  Pallas kernels  41.9 us (96%)
  local copies, waits for them, and re-layouts  1.67 us (4%)
    pallas_call x1, Pallas kernels, whole(): pl.pallas_call(functools.partial(whole_kernel, sizes), out_shape=jax.Shap...  41.9 us
    unnamed x1, local copies, waits for them, and re-layouts  1.67 us

profile of v3, /device:TPU:0, one launch (start us, length us, event | category | flops | bytes accessed | tf_op | source)
XLA Modules:
  0.0 43.6 jit_solution(14123524421456983898)
XLA Ops:
  0.0 41.9 %whole.1 = f32[16,4096]{1,0:T(8,128)} custom-call(s32[13,32]{1,0:T(8,128)} %bitcast.6, s32[16,17]{1,0:T(8,128)} %bitcast.7, s32[32,32]{1,0:T(8,128)} %relay_any.1, s32[4,32]{1,0:T(4,128)} %refs_any.1, bf16[16,4096]{1,0:T(8,128)(2,1)} %dens_any.1, f32[3,4096]{1,0:T(4,128)} %points_any.1, f32[32,128]{1,0:T(8,128)} %bitcast.5, bf16[32,64,128]{2,1,0:T(8,128)(2,1)} %basis_any.1, ...), custom_call_target="tpu_custom_call" | custom-call | tf_op jit(solution)/shard_map/whole/pallas_call | solution.py:476
  41.9 1.7 %copy.13 = f32[16,4096]{1,0:T(8,128)} copy(f32[16,4096]{1,0:T(8,128)} %whole.1) | data formatting | bytes 524288

commit v4 on v3

--- a/solution.py
+++ b/solution.py
@@ -299,14 +299,14 @@
 
     def near_leaf(leaf, carry):
         mine = row_feat[leaf]
-        field = jnp.zeros((leaf_size, rhs), jnp.float32)
         partners = [leaf + REACH + offsets_ref[slot, leaf] for slot in range(slots)]
+        kernels = []
         for first in range(0, slots, 2):
             some = partners[first : first + 2]
             cols = jnp.concatenate([col_feat[p] for p in some], axis=1)
-            vals = jnp.concatenate([values[p] for p in some], axis=1)
-            kernel = lax.rsqrt(dot(mine, cols, PLAIN)).astype(jnp.bfloat16)
-            field = field + dot(kernel, vals, ROWS_BY_ROWS)
+            kernels.append(lax.rsqrt(dot(mine, cols, PLAIN).astype(jnp.bfloat16)))
+        vals = jnp.concatenate([values[p] for p in partners], axis=1)
+        field = dot(jnp.concatenate(kernels, axis=1), vals, ROWS_BY_ROWS)
         out_ref[:, pl.ds(pl.multiple_of(leaf * leaf_size, leaf_size), leaf_size)] = field.T
         return carry
 
@@ -400,15 +400,10 @@
     loads[9].wait()
 
     def couple(blocks, store, pick, count):
-        field = jnp.zeros((rank, rhs), jnp.float32)
-        for slot in range(0, count, 4):
-            matrix = jnp.concatenate([blocks(slot + k) for k in range(4)], axis=1)
-            taken = [store[pick(slot + k)] for k in range(4)]
-            picked = jnp.concatenate(
-                [jnp.where(low, taken[0], taken[1]), jnp.where(low, taken[2], taken[3])], axis=1
-            )
-            field = field + dot(matrix, picked, ROWS_BY_ROWS)
-        return field
+        matrix = jnp.concatenate([blocks(slot) for slot in range(count)], axis=1)
+        taken = [store[pick(slot)] for slot in range(count)]
+        picked = [jnp.where(low, taken[k], taken[k + 1]) for k in range(0, count, 2)]
+        return dot(matrix, jnp.concatenate(picked, axis=1), ROWS_BY_ROWS)
 
     def one_group(group, carry):
         local1[group] = couple(

time: 43.8 us -> 43.5 us (level)
  no operation moved by 1% of the time
where the time goes in v4:
time: 43.5 us; the launch traced here: 43.3 us
  Pallas kernels  41.6 us (96%)
  local copies, waits for them, and re-layouts  1.67 us (4%)
    pallas_call x1, Pallas kernels, whole(): pl.pallas_call(functools.partial(whole_kernel, sizes), out_shape=jax.Shap...  41.6 us
    unnamed x1, local copies, waits for them, and re-layouts  1.67 us

profile of v4, /device:TPU:0, one launch (start us, length us, event | category | flops | bytes accessed | tf_op | source)
XLA Modules:
  0.0 43.3 jit_solution(13909791494222917812)
XLA Ops:
  0.0 41.6 %whole.1 = f32[16,4096]{1,0:T(8,128)} custom-call(s32[13,32]{1,0:T(8,128)} %bitcast.6, s32[16,17]{1,0:T(8,128)} %bitcast.7, s32[32,32]{1,0:T(8,128)} %relay_any.1, s32[4,32]{1,0:T(4,128)} %refs_any.1, bf16[16,4096]{1,0:T(8,128)(2,1)} %dens_any.1, f32[3,4096]{1,0:T(4,128)} %points_any.1, f32[32,128]{1,0:T(8,128)} %bitcast.5, bf16[32,64,128]{2,1,0:T(8,128)(2,1)} %basis_any.1, ...), custom_call_target="tpu_custom_call" | custom-call | tf_op jit(solution)/shard_map/whole/pallas_call | solution.py:471
  41.6 1.7 %copy.13 = f32[16,4096]{1,0:T(8,128)} copy(f32[16,4096]{1,0:T(8,128)} %whole.1) | data formatting | bytes 524288

commit v5 on v4

--- a/solution.py
+++ b/solution.py
@@ -78,6 +78,7 @@
     transfer_ref,
     coarse_coupling_ref,
     coupling_ref,
+    packed_coupling,
     row_feat,
     col_feat,
     values,
@@ -154,43 +155,43 @@
         return carry
 
     lax.fori_loop(1, total, greet, 0)
-    for load in loads[:4]:
+    for load in loads[:3]:
         load.wait()
 
     low = lax.broadcasted_iota(jnp.int32, (rhs, 2 * rank), 1) < rank
 
-    def upward(pair, carry):
+    def leaf_coefficients(step, carry):
+        for k in range(CHILDREN):
+            leaf = step * CHILDREN + k
+            start = pl.multiple_of(leaf * leaf_size, leaf_size)
+            basis = basis_ref[leaf]
+            doubled = jnp.concatenate([basis, basis], axis=0)
+            both = dot(dens_ref[:, pl.ds(start, leaf_size)], doubled, ROWS_BY_ROWS)
+            coeff[leaf] = both.astype(jnp.bfloat16)
+        return carry
+
+    lax.fori_loop(0, groups, leaf_coefficients, 0, unroll=2)
+
+    def gather(window):
+        for slot in range(half_slots):
+            first = coeff[lists_ref[slot, window]]
+            second = coeff[lists_ref[slot + half_slots, window]]
+            outgoing[window, slot] = jnp.where(low, first, second)
+
+    def parent_coefficients(pair, carry):
         parents = []
         for g in range(2):
             parent = None
             for child in range(CHILDREN):
                 leaf = (pair * 2 + g) * CHILDREN + child
-                start = pl.multiple_of(leaf * leaf_size, leaf_size)
-                basis = basis_ref[leaf]
-                doubled = jnp.concatenate([basis, basis], axis=0)
-                both = dot(dens_ref[:, pl.ds(start, leaf_size)], doubled, ROWS_BY_ROWS)
-                both = both.astype(jnp.bfloat16)
-                coeff[leaf] = both
-                term = dot(both[:, :rank], transfer_ref[leaf], PLAIN)
+                term = dot(coeff[leaf][:, :rank], transfer_ref[leaf], PLAIN)
                 parent = term if parent is None else parent + term
             parents.append(parent)
         coarse_packed[me, pair] = jnp.concatenate(parents, axis=1).astype(jnp.bfloat16)
         return carry
 
-    lax.fori_loop(0, groups // 2, upward, 0)
-
-    def gather(window, carry):
-        for slot in range(half_slots):
-            first = coeff[lists_ref[slot, window]]
-            second = coeff[lists_ref[slot + half_slots, window]]
-            outgoing[window, slot] = jnp.where(low, first, second)
-        return carry
-
-    lax.fori_loop(0, WINDOWS, gather, 0)
-    listed_packed[WINDOW] = outgoing[WINDOW]
-    for load in loads[4:9]:
+    for load in loads[3:6]:
         load.wait()
-
     pl.semaphore_wait(barrier, total - 1)
 
     def halo(side):
@@ -263,19 +264,26 @@
         return (window != WINDOW) & (other >= 0) & (other < total)
 
     def send_list(window, carry):
+        gather(window)
+
         @pl.when(in_window(window))
         def _():
             list_copy(window, 2 * WINDOW - window).start()
 
         return carry
 
+    lax.fori_loop(0, WINDOWS, send_list, 0)
+    listed_packed[WINDOW] = outgoing[WINDOW]
+    lax.fori_loop(0, groups // 2, parent_coefficients, 0)
+
     def send_inner(step, carry):
         inner_copy((my_gy + step) % n_gy, my_gy).start()
         return carry
 
     lax.fori_loop(1, n_gy, send_inner, 0)
-    lax.fori_loop(0, WINDOWS, send_list, 0)
-
+
+    for load in loads[6:9]:
+        load.wait()
     batch = 4
 
     def prepare(first_leaf, points, weights, dens, own):
@@ -399,15 +407,17 @@
     lax.fori_loop(0, total // 4, open_coarse, 0)
     loads[9].wait()
 
-    def couple(blocks, store, pick, count):
-        matrix = jnp.concatenate([blocks(slot) for slot in range(count)], axis=1)
+    def beside(blocks, count):
+        return jnp.concatenate([blocks(slot) for slot in range(count)], axis=1)
+
+    def couple(matrix, store, pick, count):
         taken = [store[pick(slot)] for slot in range(count)]
         picked = [jnp.where(low, taken[k], taken[k + 1]) for k in range(0, count, 2)]
         return dot(matrix, jnp.concatenate(picked, axis=1), ROWS_BY_ROWS)
 
     def one_group(group, carry):
         local1[group] = couple(
-            lambda s: coarse_coupling_ref[group, s],
+            beside(lambda s: coarse_coupling_ref[group, s], far1),
             coarse,
             lambda s: refs_ref[group, s],
             far1,
@@ -415,6 +425,15 @@
         return carry
 
     lax.fori_loop(0, groups, one_group, 0, unroll=2)
+
+    for group in range(groups):
+        coupling_load(group).wait()
+
+    def pack_leaf(leaf, carry):
+        packed_coupling[leaf] = beside(lambda s: coupling_ref[leaf, s], far0)
+        return carry
+
+    lax.fori_loop(0, leaf_count, pack_leaf, 0)
 
     def end_list(window, carry):
         @pl.when(in_window(window))
@@ -422,11 +441,6 @@
             list_copy(window, window).wait_recv()
             list_copy(window, 2 * WINDOW - window).wait_send()
 
-        return carry
-
-    lax.fori_loop(0, WINDOWS, end_list, 0)
-
-    def open_list(window, carry):
         for slot in range(half_slots):
             first, second = opened(listed_packed[window, slot])
             index = window * capacity + slot
@@ -434,14 +448,11 @@
             listed[index + half_slots] = second
         return carry
 
-    lax.fori_loop(0, WINDOWS, open_list, 0)
-
-    for group in range(groups):
-        coupling_load(group).wait()
+    lax.fori_loop(0, WINDOWS, end_list, 0)
 
     def one_leaf(leaf, carry):
         local0 = couple(
-            lambda s: coupling_ref[leaf, s],
+            packed_coupling[leaf],
             listed,
             lambda s: relay_ref[leaf, s],
             far0,
@@ -475,6 +486,7 @@
         out_specs=pl.BlockSpec(memory_space=pltpu.VMEM),
         scratch_shapes=held
         + [
+            pltpu.VMEM((leaf_count, rank, coupling.shape[1] * rank), half),
             pltpu.VMEM((leaf_count, leaf_size, 48), half),
             pltpu.VMEM((leaf_count + 2 * REACH, 48, leaf_size), half),
             pltpu.VMEM((leaf_count + 2 * REACH, rhs, leaf_size), half),

time: 43.5 us -> 54.8 us (1.26)
  Pallas kernels: 41.6 us -> 52.9 us
    pallas_call x1, Pallas kernels: 41.6 us -> 52.9 us  [whole(): pl.pallas_call(functools.partial(whole_kernel, sizes), out_shape=jax.Shap...]
where the time goes in v5:
time: 54.8 us; the launch traced here: 54.6 us
  Pallas kernels  52.9 us (97%)
  local copies, waits for them, and re-layouts  1.67 us (3%)
    pallas_call x1, Pallas kernels, whole(): pl.pallas_call(functools.partial(whole_kernel, sizes), out_shape=jax.Shap...  52.9 us
    unnamed x1, local copies, waits for them, and re-layouts  1.67 us

profile of v5, /device:TPU:0, one launch (start us, length us, event | category | flops | bytes accessed | tf_op | source)
XLA Modules:
  0.0 54.6 jit_solution(1625291255416253795)
XLA Ops:
  0.0 52.9 %whole.1 = f32[16,4096]{1,0:T(8,128)} custom-call(s32[13,32]{1,0:T(8,128)} %bitcast.6, s32[16,17]{1,0:T(8,128)} %bitcast.7, s32[32,32]{1,0:T(8,128)} %relay_any.1, s32[4,32]{1,0:T(4,128)} %refs_any.1, bf16[16,4096]{1,0:T(8,128)(2,1)} %dens_any.1, f32[3,4096]{1,0:T(4,128)} %points_any.1, f32[32,128]{1,0:T(8,128)} %bitcast.5, bf16[32,64,128]{2,1,0:T(8,128)(2,1)} %basis_any.1, ...), custom_call_target="tpu_custom_call" | custom-call | tf_op jit(solution)/shard_map/whole/pallas_call | solution.py:482
  52.9 1.7 %copy.13 = f32[16,4096]{1,0:T(8,128)} copy(f32[16,4096]{1,0:T(8,128)} %whole.1) | data formatting | bytes 524288

commit v6 on v5

--- a/solution.py
+++ b/solution.py
@@ -78,7 +78,6 @@
     transfer_ref,
     coarse_coupling_ref,
     coupling_ref,
-    packed_coupling,
     row_feat,
     col_feat,
     values,
@@ -407,17 +406,24 @@
     lax.fori_loop(0, total // 4, open_coarse, 0)
     loads[9].wait()
 
-    def beside(blocks, count):
-        return jnp.concatenate([blocks(slot) for slot in range(count)], axis=1)
-
-    def couple(matrix, store, pick, count):
-        taken = [store[pick(slot)] for slot in range(count)]
-        picked = [jnp.where(low, taken[k], taken[k + 1]) for k in range(0, count, 2)]
-        return dot(matrix, jnp.concatenate(picked, axis=1), ROWS_BY_ROWS)
+    def couple(blocks, store, pick, count):
+        crossed = None
+        for slot in range(0, count, 4):
+            matrix = blocks(slot).reshape(4 * rank, rank)
+            picked = jnp.concatenate([store[pick(slot + k)] for k in range(4)], axis=0)
+            term = dot(picked[:, :rank], matrix, ROWS_BY_ROWS)
+            crossed = term if crossed is None else crossed + term
+        both = jnp.zeros((rhs, 2 * rank), jnp.float32)
+        for k in range(0, 4, 2):
+            lanes = slice(k * rank, (k + 2) * rank)
+            upper = crossed[k * rhs : (k + 1) * rhs, lanes]
+            lower = crossed[(k + 1) * rhs : (k + 2) * rhs, lanes]
+            both = both + jnp.where(low, upper, lower)
+        return both[:, :rank] + both[:, rank:]
 
     def one_group(group, carry):
         local1[group] = couple(
-            beside(lambda s: coarse_coupling_ref[group, s], far1),
+            lambda s: coarse_coupling_ref[group, pl.ds(s, 4)],
             coarse,
             lambda s: refs_ref[group, s],
             far1,
@@ -428,12 +434,6 @@
 
     for group in range(groups):
         coupling_load(group).wait()
-
-    def pack_leaf(leaf, carry):
-        packed_coupling[leaf] = beside(lambda s: coupling_ref[leaf, s], far0)
-        return carry
-
-    lax.fori_loop(0, leaf_count, pack_leaf, 0)
 
     def end_list(window, carry):
         @pl.when(in_window(window))
@@ -452,13 +452,13 @@
 
     def one_leaf(leaf, carry):
         local0 = couple(
-            packed_coupling[leaf],
+            lambda s: coupling_ref[leaf, pl.ds(s, 4)],
             listed,
             lambda s: relay_ref[leaf, s],
             far0,
         )
-        downward = dot(transfer_ref[leaf], local1[leaf // CHILDREN], PLAIN)
-        field = (local0 + downward).T.astype(jnp.bfloat16)
+        downward = dot(local1[leaf // CHILDREN], transfer_ref[leaf], ROWS_BY_ROWS)
+        field = (local0 + downward).astype(jnp.bfloat16)
         span = pl.ds(pl.multiple_of(leaf * leaf_size, leaf_size), leaf_size)
         out_ref[:, span] = out_ref[:, span] + dot(field, basis_ref[leaf], PLAIN)
         return carry
@@ -486,7 +486,6 @@
         out_specs=pl.BlockSpec(memory_space=pltpu.VMEM),
         scratch_shapes=held
         + [
-            pltpu.VMEM((leaf_count, rank, coupling.shape[1] * rank), half),
             pltpu.VMEM((leaf_count, leaf_size, 48), half),
             pltpu.VMEM((leaf_count + 2 * REACH, 48, leaf_size), half),
             pltpu.VMEM((leaf_count + 2 * REACH, rhs, leaf_size), half),
@@ -496,7 +495,7 @@
             pltpu.VMEM((total, groups // 2, rhs, 2 * rank), half),
             pltpu.VMEM((WINDOWS * capacity, rhs, 2 * rank), half),
             pltpu.VMEM((total * groups, rhs, 2 * rank), half),
-            pltpu.VMEM((groups, rank, rhs), half),
+            pltpu.VMEM((groups, rhs, rank), half),
             pltpu.VMEM((2, rhs, rim), half),
             pltpu.VMEM((2, 3, rim), jnp.float32),
             pltpu.VMEM((2, REACH, leaf_size), jnp.float32),

time: 54.8 us -> 56.1 us (1.024)
  Pallas kernels: 52.9 us -> 54.2 us
    pallas_call x1, Pallas kernels: 52.9 us -> 54.2 us  [whole(): pl.pallas_call(functools.partial(whole_kernel, sizes), out_shape=jax.Shap...]
where the time goes in v6:
time: 56.1 us; the launch traced here: 55.9 us
  Pallas kernels  54.2 us (97%)
  local copies, waits for them, and re-layouts  1.67 us (3%)
    pallas_call x1, Pallas kernels, whole(): pl.pallas_call(functools.partial(whole_kernel, sizes), out_shape=jax.Shap...  54.2 us
    unnamed x1, local copies, waits for them, and re-layouts  1.67 us

profile of v6, /device:TPU:0, one launch (start us, length us, event | category | flops | bytes accessed | tf_op | source)
XLA Modules:
  0.0 55.9 jit_solution(5029570648315957208)
XLA Ops:
  0.0 54.2 %whole.1 = f32[16,4096]{1,0:T(8,128)} custom-call(s32[13,32]{1,0:T(8,128)} %bitcast.6, s32[16,17]{1,0:T(8,128)} %bitcast.7, s32[32,32]{1,0:T(8,128)} %relay_any.1, s32[4,32]{1,0:T(4,128)} %refs_any.1, bf16[16,4096]{1,0:T(8,128)(2,1)} %dens_any.1, f32[3,4096]{1,0:T(4,128)} %points_any.1, f32[32,128]{1,0:T(8,128)} %bitcast.5, bf16[32,64,128]{2,1,0:T(8,128)(2,1)} %basis_any.1, ...), custom_call_target="tpu_custom_call" | custom-call | tf_op jit(solution)/shard_map/whole/pallas_call | solution.py:482
  54.2 1.7 %copy.13 = f32[16,4096]{1,0:T(8,128)} copy(f32[16,4096]{1,0:T(8,128)} %whole.1) | data formatting | bytes 524288

commit v7 on v6

--- a/solution.py
+++ b/solution.py
@@ -191,6 +191,7 @@
 
     for load in loads[3:6]:
         load.wait()
+    lax.fori_loop(0, groups // 2, parent_coefficients, 0)
     pl.semaphore_wait(barrier, total - 1)
 
     def halo(side):
@@ -271,15 +272,13 @@
 
         return carry
 
+    def send_inner(step, carry):
+        inner_copy((my_gy + step) % n_gy, my_gy).start()
+        return carry
+
+    lax.fori_loop(1, n_gy, send_inner, 0)
     lax.fori_loop(0, WINDOWS, send_list, 0)
     listed_packed[WINDOW] = outgoing[WINDOW]
-    lax.fori_loop(0, groups // 2, parent_coefficients, 0)
-
-    def send_inner(step, carry):
-        inner_copy((my_gy + step) % n_gy, my_gy).start()
-        return carry
-
-    lax.fori_loop(1, n_gy, send_inner, 0)
 
     for load in loads[6:9]:
         load.wait()

time: 56.1 us -> 48.2 us (0.86)
  Pallas kernels: 54.2 us -> 46.3 us
    pallas_call x1, Pallas kernels: 54.2 us -> 46.3 us  [whole(): pl.pallas_call(functools.partial(whole_kernel, sizes), out_shape=jax.Shap...]
where the time goes in v7:
time: 48.2 us; the launch traced here: 48 us
  Pallas kernels  46.3 us (96%)
  local copies, waits for them, and re-layouts  1.67 us (3%)
    pallas_call x1, Pallas kernels, whole(): pl.pallas_call(functools.partial(whole_kernel, sizes), out_shape=jax.Shap...  46.3 us
    unnamed x1, local copies, waits for them, and re-layouts  1.67 us

profile of v7, /device:TPU:0, one launch (start us, length us, event | category | flops | bytes accessed | tf_op | source)
XLA Modules:
  0.0 48.0 jit_solution(4825453257113713714)
XLA Ops:
  0.0 46.3 %whole.1 = f32[16,4096]{1,0:T(8,128)} custom-call(s32[13,32]{1,0:T(8,128)} %bitcast.6, s32[16,17]{1,0:T(8,128)} %bitcast.7, s32[32,32]{1,0:T(8,128)} %relay_any.1, s32[4,32]{1,0:T(4,128)} %refs_any.1, bf16[16,4096]{1,0:T(8,128)(2,1)} %dens_any.1, f32[3,4096]{1,0:T(4,128)} %points_any.1, f32[32,128]{1,0:T(8,128)} %bitcast.5, bf16[32,64,128]{2,1,0:T(8,128)(2,1)} %basis_any.1, ...), custom_call_target="tpu_custom_call" | custom-call | tf_op jit(solution)/shard_map/whole/pallas_call | solution.py:481
  46.3 1.7 %copy.13 = f32[16,4096]{1,0:T(8,128)} copy(f32[16,4096]{1,0:T(8,128)} %whole.1) | data formatting | bytes 524288
